TPU v7x, 32 devices: a whole 2x2x4 slice. The times are simulated.
32 devices in a mesh: lib: 2 (over x), hit: 8 (over z, y), lm: 2 (over core).
Axes of the slice: x: 2, y: 2, z: 4, core: 2. Of those that a mesh axis runs over, the one named last changes fastest.
Arguments:
- fingerprints: int32 [8192, 128], P(('lib', 'hit')), parts along dimension 0, may hold values from 0 to 65535, as said below
- pick_list: int32 [8192], P(('lib', 'lm')), parts along dimension 0, may hold values from 0 to 4095, as said below
- inverse_root: bfloat16 [8192, 2, 2048], P('lib', 'lm', 'hit'), parts along dimension 0, may hold values from -0.09375 to 0.09375
Outputs:
- embedding: bfloat16 [8192, 4096], P(('lib', 'hit'), 'lm'), parts along dimension 0
There are 2 independent parts, one for each index of `lib`. A program takes and returns all parts, laid end to end along the dimension named above; each array names one. Nothing has to cross between parts.
Inputs may be any that keep to these rules, and one draw needn't show every extreme that they name: `pick_list`: within each half of the list, at most 768 picks lie in any one aligned block of 512 hits, and exactly 768 lie in one such block. `fingerprints`: every fingerprint has the lowest bit of its first word set.
All inputs are finite; a program needn't handle non-finite values.
Results may differ from a plain program's by a relative error of at most 0.0049.
Values may be sent and summed in bfloat16 or wider, within the bound.
No kernel may reach another device: no remote copies, remote signals or barrier semaphores. Data moves between devices by JAX's collectives and lax.ppermute only.
A program may use at most 128 MiB of HBM per device.

v0:
```python
import functools

import jax
import jax.numpy as jnp
from jax import lax
from jax.experimental import pallas as pl
from jax.experimental.pallas import tpu as pltpu
from jax.sharding import PartitionSpec as P

F8 = jnp.float8_e4m3fn
BITS = 16
VMEM = pl.BlockSpec(memory_space=pltpu.VMEM)
ANY = pl.BlockSpec(memory_space=pl.ANY)


def unpack_kernel(*refs, count, stack, single, inputs):
    bits_ref, count_ref = refs[inputs : inputs + 2]
    more = refs[inputs + 2 :]
    word_ref = refs[0]
    if stack:
        word_ref = more[0]
        for at in range(count):
            word_ref[at] = refs[at][...]
    if single:
        for at in range(count):
            more[at - count][...] = word_ref[at]

    @pl.loop(0, count)
    def _(at):
        words = word_ref[at].astype(jnp.int32)
        rows, width = words.shape
        here = pl.ds(pl.multiple_of(at * rows, rows), rows)
        ones = jnp.sum(lax.population_count(words).astype(jnp.float32), axis=1, keepdims=True)
        count_ref[here, :] = jnp.broadcast_to(ones, (rows, count_ref.shape[1]))
        for bit in range(BITS):
            flag = ((words >> bit) & 1).astype(jnp.int8)
            bits_ref[here, bit * width : (bit + 1) * width] = flag.astype(F8)


def unpack(words, after=(), stack=False, single=False):
    words = list(words) if isinstance(words, (list, tuple)) else [words]
    rows, width = words[0].shape[-2:]
    count = words[0].shape[0] if len(words[0].shape) == 3 else len(words)
    shapes = [
        jax.ShapeDtypeStruct((count * rows, BITS * width), F8),
        jax.ShapeDtypeStruct((count * rows, 128), jnp.float32),
    ]
    if stack:
        shapes.append(jax.ShapeDtypeStruct((count, rows, width), words[0].dtype))
    if single:
        shapes += [jax.ShapeDtypeStruct((rows, width), words[0].dtype)] * count
    out = pl.pallas_call(
        functools.partial(
            unpack_kernel,
            count=count,
            stack=stack,
            single=single,
            inputs=len(words) + len(after),
        ),
        in_specs=[VMEM] * len(words) + [ANY] * len(after),
        out_specs=[VMEM] * len(shapes),
        out_shape=shapes,
        compiler_params=pltpu.CompilerParams(vmem_limit_bytes=24 * 2**20),
        cost_estimate=pl.CostEstimate(
            flops=4096 * count * rows * BITS * width, bytes_accessed=rows * width, transcendentals=0
        ),
        name="unpack",
    )(*words, *after)
    return tuple(out[:2]), out[2:]


def spread_kernel(mine_ref, own_ref, other_ref, sib_ref, *refs, steps, hit_rows, chunk):
    out_ref = refs[-1]
    cols = own_ref.shape[1]
    half = mine_ref.shape[1]
    rows = hit_rows // 2
    side = lax.axis_index("lm")
    me = lax.axis_index("hit")
    places = []
    for place in (side, 1 - side):
        for start in range(0, half, chunk):
            at = pl.ds(pl.multiple_of(place * half + start, chunk), chunk)
            places.append((start, at))
    parts = [
        lax.broadcasted_iota(jnp.int32, (rows, 1), 0) + ((me ^ k) * hit_rows + side * rows)
        for k in steps
    ]
    ids = jnp.concatenate(parts, axis=0)
    own = sib = None
    for i, (start, at) in enumerate(places):
        pick_ref = mine_ref if i < len(places) // 2 else other_ref
        hot = jnp.where(pick_ref[0:1, start : start + chunk] == ids, 1.0, 0.0).astype(jnp.bfloat16)
        part = jnp.dot(hot, sib_ref[at, :], preferred_element_type=jnp.float32)
        sib = part if sib is None else sib + part
        part = jnp.dot(hot, own_ref[at, :], preferred_element_type=jnp.float32)
        own = part if own is None else own + part
    out_ref[:cols, :] = own.T.astype(jnp.bfloat16)
    out_ref[cols:, :] = sib.T.astype(jnp.bfloat16)


def spread(steps, hit_rows, mine, own, other, sib, after):
    marks, cols = own.shape
    hits = len(steps) * hit_rows // 2
    chunk = 512
    return pl.pallas_call(
        functools.partial(spread_kernel, steps=steps, hit_rows=hit_rows, chunk=chunk),
        in_specs=[VMEM] * 4 + [ANY] * len(after),
        out_specs=VMEM,
        out_shape=jax.ShapeDtypeStruct((2 * cols, hits), jnp.bfloat16),
        compiler_params=pltpu.CompilerParams(vmem_limit_bytes=24 * 2**20),
        cost_estimate=pl.CostEstimate(
            flops=marks * cols * hits // 8, bytes_accessed=marks * cols, transcendentals=0
        ),
        name="spread",
    )(mine, own, other, sib, *after)


def block_kernel(words_ref, *refs, sums, pairs, tile):
    later_ref, both_ref, own_ref, sib_ref, flags, kern = refs[-6:]
    sum_refs = refs[:sums]
    pair_refs = refs[sums : sums + 2 * pairs]
    held = refs[sums + 2 * pairs : sums + 2 * pairs + 2]
    later_ref[0] = held[0][...]
    later_ref[1] = held[1][...]
    words = words_ref[...].astype(jnp.int32).T
    width = words.shape[0]
    count = jnp.sum(lax.population_count(words).astype(jnp.float32), axis=0, keepdims=True)
    for bit in range(BITS):
        flag = ((words >> bit) & 1).astype(jnp.int8)
        flags[bit * width : (bit + 1) * width, :] = flag.astype(F8)
    at = 0
    for bits_ref, count_ref in zip(pair_refs[::2], pair_refs[1::2]):
        rows = bits_ref.shape[0]
        size = min(tile, rows)
        for low in range(0, rows, size):
            here = slice(low, low + size)
            common = jnp.dot(bits_ref[here, :], flags[...], preferred_element_type=jnp.float32)
            union = (count + count_ref[here, 0:1]) - common
            kern[at : at + size, :] = (common / union).astype(jnp.bfloat16)
            at += size
    at = 0
    made = []
    for ref in sum_refs:
        rows = ref.shape[1]
        made.append(
            jnp.dot(ref[...], kern[at : at + rows, :], preferred_element_type=jnp.float32)
        )
        at += rows
    mine = sum(made[: sums // 2])
    theirs = sum(made[sums // 2 :])
    cols = mine.shape[0] // 2
    own = (mine[:cols] + theirs[cols:]).T.astype(jnp.bfloat16)
    sib = (mine[cols:] + theirs[:cols]).T.astype(jnp.bfloat16)
    both_ref[0] = own
    both_ref[1] = sib
    own_ref[...] = own
    sib_ref[...] = sib


def block(words, sums, pairs, held, after):
    rows, width = words.shape
    cols = sums[0].shape[0] // 2
    hits = sum(x.shape[1] for x in sums)
    flat = [x for pair in pairs for x in pair] + list(held)
    one = jax.ShapeDtypeStruct((rows, cols), jnp.bfloat16)
    both = jax.ShapeDtypeStruct((2, rows, cols), jnp.bfloat16)
    return pl.pallas_call(
        functools.partial(block_kernel, sums=len(sums), pairs=len(pairs), tile=512),
        in_specs=[VMEM] * (1 + len(sums) + len(flat)) + [ANY] * len(after),
        out_specs=[VMEM] * 4,
        out_shape=[both, both, one, one],
        scratch_shapes=[
            pltpu.VMEM((BITS * width, rows), F8),
            pltpu.VMEM((hits, rows), jnp.bfloat16),
        ],
        compiler_params=pltpu.CompilerParams(vmem_limit_bytes=32 * 2**20),
        cost_estimate=pl.CostEstimate(
            flops=2 * hits * rows * (BITS * width + 2 * cols),
            bytes_accessed=rows * cols,
            transcendentals=0,
        ),
        name="block",
    )(words, *sums, *flat, *after)


def fill_kernel(*refs, steps):
    out_ref = refs[-1]
    side = lax.axis_index("lm")
    me = lax.axis_index("hit")
    for i, k in enumerate(steps):
        for at, which in ((0, side), (1, 1 - side)):
            ref = refs[2 * i + at]
            piece = ref[at] if len(ref.shape) == 3 else ref[...]
            rows, cols = piece.shape
            row = pl.ds(pl.multiple_of(which * rows, rows), rows)
            out_ref[row, pl.ds(pl.multiple_of((me ^ k) * cols, cols), cols)] = piece


def fill(steps, pieces, shape, after):
    return pl.pallas_call(
        functools.partial(fill_kernel, steps=steps),
        in_specs=[VMEM] * (2 * len(pieces)) + [ANY] * len(after),
        out_specs=VMEM,
        out_shape=jax.ShapeDtypeStruct(shape, jnp.bfloat16),
        compiler_params=pltpu.CompilerParams(vmem_limit_bytes=16 * 2**20),
        name="fill",
    )(*[x for piece in pieces for x in piece], *after)


def small(fingerprints, pick_list, inverse_root):
    hit_rows, width = fingerprints.shape
    devices = lax.axis_size("hit")
    side = lax.axis_index("lm")
    half = hit_rows // 2
    weight = inverse_root[:, 0, :]
    cols = weight.shape[1]

    def across(x, k):
        return lax.ppermute(x, "hit", [(i, i ^ k) for i in range(devices)])

    def over(x):
        return lax.ppermute(x, "lm", [(0, 1), (1, 0)])

    mine = lax.dynamic_slice_in_dim(fingerprints, side * half, half).astype(jnp.uint16)
    other_picks = over(pick_list)
    other_weight = over(weight)

    even = list(range(0, devices, 2))
    odd = [k ^ 1 for k in even]
    words_z = [across(mine, k) if k else mine for k in even]

    args = (hit_rows, pick_list.reshape(1, -1), weight, other_picks.reshape(1, -1), other_weight)
    sums = [spread(even, *args, [])]
    pair_even, (words_even, *list_even) = unpack(words_z, sums, True, True)
    words_odd = across(words_even, 1)
    sums.append(spread(odd, *args, [words_even]))
    sums += [over(x) for x in sums]
    pair_odd, list_odd = unpack(words_odd, single=True)
    pairs = [pair_even, pair_odd, unpack(over(words_even))[0], unpack(over(words_odd))[0]]
    words = dict(zip(even + odd, [*list_even, *list_odd]))

    order = list(range(devices - 1, -1, -1))
    direct, hands, waits = order[:-1], {}, {}
    if devices == 8:
        order = [7, 6, 4, 5, 3, 2, 1, 0]
        direct = [7, 6, 5, 3, 2, 1]
        hands = {3: 4}
        waits = {2: [7], 1: [6]}
    halves = dict()
    pieces = dict()
    got = dict()
    out = (sums[0],) * 4
    held = (sums[0][:half, :cols],) * 2
    for k in order:
        after = list(out) + [got[x] for x in waits.get(k, [])]
        after += [out[0]] * (6 - len(after))
        if k in hands:
            held = halves[hands[k]]
        later, made, *last = out = block(words[k], sums, pairs, held, after)
        held = last
        if k in hands:
            x = hands[k]
            got[x] = across(later, x)
            pieces[x] = (got[x], got[x])
        if k in direct:
            got[k] = across(made, k)
            pieces[k] = (got[k], over(got[k][1]))
        else:
            halves[k] = (last[0], over(last[1]))
    pieces[0] = halves[0]
    return fill(order, [pieces[k] for k in order], (hit_rows, devices * cols), out[:2])


def large(fingerprints, pick_list, inverse_root):
    hit_rows, width = fingerprints.shape
    devices = lax.axis_size("hit")
    side = lax.axis_index("lm")
    half = hit_rows // 2
    weight = inverse_root[:, 0, :]
    cols = weight.shape[1]
    picks = lax.all_gather(pick_list, "lm", tiled=True)
    words = lax.all_gather(fingerprints, "hit", tiled=True)
    hits = words.shape[0]
    blocks = words.reshape(devices, hit_rows, width)

    def spread_block(index):
        hot = (index * hit_rows + jnp.arange(hit_rows))[:, None] == picks[None, :]
        made = jnp.dot(hot.astype(jnp.bfloat16), weight, preferred_element_type=jnp.float32)
        return made.astype(jnp.bfloat16)

    def flag_block(block_words):
        flags = [((block_words >> bit) & 1).astype(F8) for bit in range(BITS)]
        return jnp.concatenate(flags, axis=1)

    sums = lax.map(spread_block, jnp.arange(devices)).reshape(hits, cols)
    sums = lax.all_gather(sums, "lm", axis=1, tiled=True)
    bits = lax.map(flag_block, blocks).reshape(hits, BITS * width)
    count = jnp.sum(lax.population_count(words), axis=1).astype(jnp.float32)

    def one(index):
        start = index * hit_rows + side * half
        rows = lax.dynamic_slice_in_dim(bits, start, half)
        common = lax.dot_general(
            rows, bits, (((1,), (1,)), ((), ())), preferred_element_type=jnp.float32
        )
        union = lax.dynamic_slice_in_dim(count, start, half)[:, None] + count[None, :] - common
        kernel = (common / union).astype(jnp.bfloat16)
        return jnp.dot(kernel, sums, preferred_element_type=jnp.float32).astype(jnp.bfloat16)

    made = lax.map(one, jnp.arange(devices))
    got = lax.all_to_all(made, "hit", 0, 0, tiled=True)
    got = got.reshape(devices, half, 2, cols).transpose(2, 1, 0, 3)
    got = got.reshape(2, 1, half, devices * cols)
    return lax.all_to_all(got, "lm", 0, 1, tiled=True).reshape(hit_rows, devices * cols)


def local(fingerprints, pick_list, inverse_root):
    if lax.axis_size("hit") > 8:
        return large(fingerprints, pick_list, inverse_root)
    return small(fingerprints, pick_list, inverse_root)


def solution(mesh):
    placed = (P(("lib", "hit"), None), P(("lib", "lm")), P("lib", "lm", "hit"))
    return jax.shard_map(
        local, mesh=mesh, in_specs=placed, out_specs=P(("lib", "hit"), "lm"), check_vma=False
    )
```

profile of v0, /device:TPU:0, one launch (start us, length us, event | category | flops | bytes accessed | tf_op | source)
XLA Modules:
  0.0 84.6 jit_solution(787958245429529570)
XLA Ops:
  0.0 0.5 collective-permute-start.4
  0.5 0.9 %dynamic-slice_convert_fusion.refs_0_ = u16[256,128]{1,0:T(8,128)(2,1)S(1)} fusion(s32[512,128]{1,0:T(8,128)} %param.3, s32[]{:T(128)S(6)} %select_n.3), kind=kLoop, calls=%fused_computation.6 | loop fusion | flops 32768 | bytes 196612 | tf_op jit(solution)/shard_map/convert_element_type | solution.py:224
  1.4 2.6 %collective-permute-start = (u16[256,128]{1,0:T(8,128)(2,1)S(1)}, u16[256,128]{1,0:T(8,128)(2,1)S(1)}, u32[]{:S(2)}, u32[]{:S(2)}) collective-permute-start(u16[256,128]{1,0:T(8,128)(2,1)S(1)} %dynamic-slice_convert_fusion.refs_0_), channel_id=1, source_target_pairs={{0,4},{2,6},{4,0},{6,2},{8,12},{10,14},{12,8},{14,10},{1,5},{3,7},... | collective-permute-start | bytes 196616 | tf_op jit(solution)/shard_map/ppermute | solution.py:219
  4.0 2.6 %collective-permute-start.1 = (u16[256,128]{1,0:T(8,128)(2,1)S(1)}, u16[256,128]{1,0:T(8,128)(2,1)S(1)}, u32[]{:S(2)}, u32[]{:S(2)}) collective-permute-start(u16[256,128]{1,0:T(8,128)(2,1)S(1)} %dynamic-slice_convert_fusion.refs_0_), channel_id=1, source_target_pairs={{0,8},{2,10},{4,12},{6,14},{8,0},{10,2},{12,4},{14,6},{1,9},{3,11}... | collective-permute-start | bytes 196616 | tf_op jit(solution)/shard_map/ppermute | solution.py:219
  6.6 0.0 collective-permute-start.2
  6.6 0.0 collective-permute-start.3
  6.6 1.4 %collective-permute-done.3 = s32[2048]{0:T(1024)S(1)} collective-permute-done((s32[2048]{0:T(1024)}, s32[2048]{0:T(1024)S(1)}, u32[]{:S(2)}, u32[]{:S(2)}) %collective-permute-start.3) | collective-permute-done | bytes 8224 | tf_op jit(solution)/shard_map/ppermute | solution.py:222
  8.0 0.0 collective-permute-done.4.sib_ref
  8.0 1.6 %copy-done = bf16[4096,1,256]{2,0,1:T(8,128)(2,1)S(1)} copy-done((bf16[4096,1,256]{2,0,1:T(8,128)(2,1)S(1)}, bf16[4096,1,256]{2,0,1:T(8,128)(2,1)}, u32[]{:S(2)}) %copy-start) | copy-done | bytes 2097176
  9.6 0.7 copy-done.2
  10.3 4.6 %spread.2.refs_4_.refs_0_.refs_14_.refs_15_.refs_16_.refs_17_.refs_18_.refs_19_ = bf16[512,1024]{1,0:T(8,128)(2,1)S(1)} custom-call(s32[1,2048]{1,0:T(1,128)S(1)} %bitcast.18, bf16[4096,256]{1,0:T(8,128)(2,1)S(1)} %bitcast.16, s32[1,2048]{1,0:T(1,128)S(1)} %bitcast.20, bf16[4096,256]{1,0:T(8,128)(2,1)S(1)} %collective-permute-done.4.sib_ref), custom_call_target="tpu_custom_call" | custom-call | flops 134217728 | bytes 1048576 | tf_op jit(solution)/shard_map/spread/pallas_call | solution.py:105
  14.9 0.0 copy-start.1
  14.9 0.0 collective-permute-done.refs_1_
  15.0 0.0 collective-permute-done.1.refs_2_
  15.0 0.0 collective-permute-done.2.refs_3_
  15.0 1.2 %unpack.4 = (f8e4m3fn[1024,2048]{1,0:T(32,128)(4,1)S(1)}, f32[1024,128]{1,0:T(8,128)S(1)}, u16[4,256,128]{2,1,0:T(8,128)(2,1)S(1)}, u16[256,128]{1,0:T(8,128)(2,...) custom-call(u16[256,128]{1,0:T(8,128)(2,1)S(1)} %dynamic-slice_convert_fusion.refs_0_,, ...), custom_call_target="tpu_custom_call" | custom-call | flops 8589934592 | bytes 32768 | tf_op jit(solution)/shard_map/unpack/pallas_call | solution.py:52
  16.2 1.8 %collective-permute-start.5 = (u16[4,256,128]{2,1,0:T(8,128)(2,1)S(1)}, u16[4,256,128]{2,1,0:T(8,128)(2,1)S(1)}, u32[]{:S(2)}, u32[]{:S(2)}) collective-permute-start(u16[4,256,128]{2,1,0:T(8,128)(2,1)S(1)} %get-tuple-element.54.refs_0_), channel_id=1, source_target_pairs={{0,2},{2,0},{4,6},{6,4},{8,10},{10,8},{12,14},{14,12},{1,3},{3,1},... | collective-permute-start | bytes 786440 | tf_op jit(solution)/shard_map/ppermute | solution.py:219
  17.9 0.0 collective-permute-start.8
  17.9 0.5 collective-permute-start.6
  18.5 4.6 %spread.3.refs_1_ = bf16[512,1024]{1,0:T(8,128)(2,1)S(1)} custom-call(s32[1,2048]{1,0:T(1,128)S(1)} %bitcast.19, bf16[4096,256]{1,0:T(8,128)(2,1)S(1)} %bitcast.17, s32[1,2048]{1,0:T(1,128)S(1)} %bitcast.21, bf16[4096,256]{1,0:T(8,128)(2,1)S(1)} %collective-permute-done.4.sib_ref, u16[4,256,128]{2,1,0:T(8,128)(2,1)S(1)} %get-tuple-element.54.refs_0_), custom_call_target="tpu_custom_call" | custom-call | flops 134217728 | bytes 1048576 | tf_op jit(solution)/shard_map/spread/pallas_call | solution.py:105
  23.1 0.1 collective-permute-start.7
  23.2 1.4 %collective-permute-done.5.refs_0_ = u16[4,256,128]{2,1,0:T(8,128)(2,1)S(1)} collective-permute-done((u16[4,256,128]{2,1,0:T(8,128)(2,1)S(1)}, u16[4,256,128]{2,1,0:T(8,128)(2,1)S(1)}, u32[]{:S(2)}, u32[]{:S(2)}) %collective-permute-start.5) | collective-permute-done | bytes 262176 | tf_op jit(solution)/shard_map/ppermute | solution.py:219
  24.6 1.2 %unpack.5 = (f8e4m3fn[1024,2048]{1,0:T(32,128)(4,1)S(1)}, f32[1024,128]{1,0:T(8,128)S(1)}, u16[256,128]{1,0:T(8,128)(2,1)S(1)}, u16[256,128]{1,0:T(8,128)(2,1)S(...) custom-call(u16[4,256,128]{2,1,0:T(8,128)(2,1)S(1)} %collective-permute-done.5.refs_0_), custom_call_target="tpu_custom_call" | custom-call | flops 8589934592 | bytes 32768 | tf_op jit(solution)/shard_map/unpack/pallas_call | solution.py:52
  25.7 0.0 collective-permute-start.9
  25.8 0.0 collective-permute-done.8.refs_0_
  25.8 1.1 %unpack.6 = (f8e4m3fn[1024,2048]{1,0:T(32,128)(4,1)S(1)}, f32[1024,128]{1,0:T(8,128)S(1)}) custom-call(u16[4,256,128]{2,1,0:T(8,128)(2,1)S(1)} %collective-permute-done.8.refs_0_), custom_call_target="tpu_custom_call" | custom-call | flops 8589934592 | bytes 32768 | tf_op jit(solution)/shard_map/unpack/pallas_call | solution.py:52
  26.9 0.4 collective-permute-done.9.refs_0_
  27.3 1.3 %unpack.7 = (f8e4m3fn[1024,2048]{1,0:T(32,128)(4,1)S(1)}, f32[1024,128]{1,0:T(8,128)S(1)}) custom-call(u16[4,256,128]{2,1,0:T(8,128)(2,1)S(1)} %collective-permute-done.9.refs_0_), custom_call_target="tpu_custom_call" | custom-call | flops 8589934592 | bytes 32768 | tf_op jit(solution)/shard_map/unpack/pallas_call | solution.py:52
  28.6 0.0 collective-permute-done.7.refs_3_
  28.6 0.0 collective-permute-done.6.refs_2_
  28.6 3.8 %block.8 = (bf16[2,256,256]{2,1,0:T(8,128)(2,1)S(1)}, bf16[2,256,256]{2,1,0:T(8,128)(2,1)S(1)}, bf16[256,256]{1,0:T(8,128)(2,1)S(1)}, bf16[256,256]{1,0:T(8,128)(2,1)S(1)}) custom-call(u16[256,128]{1,0:T(8,128)(2,1)S(1)} %get-tuple-element.55.words_ref, bf16[512,1024]{1,0:T(8,128)(2,1)S(1)} %spread.2.refs_4_.refs_0_.refs_14_.refs_15_.refs_16_.refs_17_.refs_18_.refs_19_, ...), custom_call_target="tpu_custom_call" | custom-call | flops 5368709120 | bytes 65536 | tf_op jit(solution)/shard_map/block/pallas_call | solution.py:167
  32.4 4.8 %collective-permute-start.10 = (bf16[2,256,256]{2,1,0:T(8,128)(2,1)S(1)}, bf16[2,256,256]{2,1,0:T(8,128)(2,1)S(1)}, u32[]{:S(2)}, u32[]{:S(2)}) collective-permute-start(bf16[2,256,256]{2,1,0:T(8,128)(2,1)S(1)} %get-tuple-element.64.refs_15_), channel_id=1, source_target_pairs={{0,14},{2,12},{4,10},{6,8},{8,6},{10,4},{12,2},{14,0},{1,15},{3,13... | collective-permute-start | bytes 786440 | tf_op jit(solution)/shard_map/ppermute | solution.py:219
  37.2 3.8 %block.9 = (bf16[2,256,256]{2,1,0:T(8,128)(2,1)S(1)}, bf16[2,256,256]{2,1,0:T(8,128)(2,1)S(1)}, bf16[256,256]{1,0:T(8,128)(2,1)S(1)}, bf16[256,256]{1,0:T(8,128)(2,1)S(1)}) custom-call(u16[256,128]{1,0:T(8,128)(2,1)S(1)} %get-tuple-element.65.words_ref, bf16[512,1024]{1,0:T(8,128)(2,1)S(1)} %spread.2.refs_4_.refs_0_.refs_14_.refs_15_.refs_16_.refs_17_.refs_18_.refs_19_, ...), custom_call_target="tpu_custom_call" | custom-call | flops 5368709120 | bytes 65536 | tf_op jit(solution)/shard_map/block/pallas_call | solution.py:167
  41.0 0.3 collective-permute-start.12
  41.3 3.8 %block.10 = (bf16[2,256,256]{2,1,0:T(8,128)(2,1)S(1)}, bf16[2,256,256]{2,1,0:T(8,128)(2,1)S(1)}, bf16[256,256]{1,0:T(8,128)(2,1)S(1)}, bf16[256,256]{1,0:T(8,128)(2,1)S(1)}) custom-call(u16[256,128]{1,0:T(8,128)(2,1)S(1)} %get-tuple-element.71.words_ref, bf16[512,1024]{1,0:T(8,128)(2,1)S(1)} %spread.2.refs_4_.refs_0_.refs_14_.refs_15_.refs_16_.refs_17_.refs_18_.refs_19_, ...), custom_call_target="tpu_custom_call" | custom-call | flops 5368709120 | bytes 65536 | tf_op jit(solution)/shard_map/block/pallas_call | solution.py:167
  45.0 0.1 collective-permute-start.14
  45.1 4.0 %block.11 = (bf16[2,256,256]{2,1,0:T(8,128)(2,1)S(1)}, bf16[2,256,256]{2,1,0:T(8,128)(2,1)S(1)}, bf16[256,256]{1,0:T(8,128)(2,1)S(1)}, bf16[256,256]{1,0:T(8,128)(2,1)S(1)}) custom-call(u16[256,128]{1,0:T(8,128)(2,1)S(1)} %get-tuple-element.77.words_ref, bf16[512,1024]{1,0:T(8,128)(2,1)S(1)} %spread.2.refs_4_.refs_0_.refs_14_.refs_15_.refs_16_.refs_17_.refs_18_.refs_19_, ...), custom_call_target="tpu_custom_call" | custom-call | flops 5368709120 | bytes 65536 | tf_op jit(solution)/shard_map/block/pallas_call | solution.py:167
  49.1 0.1 collective-permute-start.16
  49.2 0.0 collective-permute-done.14.refs_13_
  49.2 3.8 %block.12 = (bf16[2,256,256]{2,1,0:T(8,128)(2,1)S(1)}, bf16[2,256,256]{2,1,0:T(8,128)(2,1)S(1)}, bf16[256,256]{1,0:T(8,128)(2,1)S(1)}, bf16[256,256]{1,0:T(8,128)(2,1)S(1)}) custom-call(u16[256,128]{1,0:T(8,128)(2,1)S(1)} %get-tuple-element.70.words_ref, bf16[512,1024]{1,0:T(8,128)(2,1)S(1)} %spread.2.refs_4_.refs_0_.refs_14_.refs_15_.refs_16_.refs_17_.refs_18_.refs_19_, ...), custom_call_target="tpu_custom_call" | custom-call | flops 5368709120 | bytes 65536 | tf_op jit(solution)/shard_map/block/pallas_call | solution.py:167
  53.0 5.1 %collective-permute-start.18 = (bf16[2,256,256]{2,1,0:T(8,128)(2,1)S(1)}, bf16[2,256,256]{2,1,0:T(8,128)(2,1)S(1)}, u32[]{:S(2)}, u32[]{:S(2)}) collective-permute-start(bf16[2,256,256]{2,1,0:T(8,128)(2,1)S(1)} %get-tuple-element.85.refs_15_), channel_id=1, source_target_pairs={{0,6},{2,4},{4,2},{6,0},{8,14},{10,12},{12,10},{14,8},{1,7},{3,5},... | collective-permute-start | bytes 786440 | tf_op jit(solution)/shard_map/ppermute | solution.py:219
  58.1 0.0 collective-permute-start.15
  58.1 0.0 collective-permute-done.10.refs_18_.refs_0_
  58.1 3.8 %block.13 = (bf16[2,256,256]{2,1,0:T(8,128)(2,1)S(1)}, bf16[2,256,256]{2,1,0:T(8,128)(2,1)S(1)}, bf16[256,256]{1,0:T(8,128)(2,1)S(1)}, bf16[256,256]{1,0:T(8,128)(2,1)S(1)}) custom-call(u16[256,128]{1,0:T(8,128)(2,1)S(1)} %get-tuple-element.86.words_ref, bf16[512,1024]{1,0:T(8,128)(2,1)S(1)} %spread.2.refs_4_.refs_0_.refs_14_.refs_15_.refs_16_.refs_17_.refs_18_.refs_19_, ...), custom_call_target="tpu_custom_call" | custom-call | flops 5368709120 | bytes 65536 | tf_op jit(solution)/shard_map/block/pallas_call | solution.py:167
  61.9 1.3 %collective-permute-start.20 = (bf16[2,256,256]{2,1,0:T(8,128)(2,1)S(1)}, bf16[2,256,256]{2,1,0:T(8,128)(2,1)S(1)}, u32[]{:S(2)}, u32[]{:S(2)}) collective-permute-start(bf16[2,256,256]{2,1,0:T(8,128)(2,1)S(1)} %get-tuple-element.89.refs_15_), channel_id=1, source_target_pairs={{0,4},{2,6},{4,0},{6,2},{8,12},{10,14},{12,8},{14,10},{1,5},{3,7},... | collective-permute-start | bytes 786440 | tf_op jit(solution)/shard_map/ppermute | solution.py:219
  63.2 0.0 collective-permute-done.12.refs_18_.refs_2_
  63.2 3.8 %block.14 = (bf16[2,256,256]{2,1,0:T(8,128)(2,1)S(1)}, bf16[2,256,256]{2,1,0:T(8,128)(2,1)S(1)}, bf16[256,256]{1,0:T(8,128)(2,1)S(1)}, bf16[256,256]{1,0:T(8,128)(2,1)S(1)}) custom-call(u16[256,128]{1,0:T(8,128)(2,1)S(1)} %get-tuple-element.90.words_ref, bf16[512,1024]{1,0:T(8,128)(2,1)S(1)} %spread.2.refs_4_.refs_0_.refs_14_.refs_15_.refs_16_.refs_17_.refs_18_.refs_19_, ...), custom_call_target="tpu_custom_call" | custom-call | flops 5368709120 | bytes 65536 | tf_op jit(solution)/shard_map/block/pallas_call | solution.py:167
  67.0 0.6 collective-permute-start.22
  67.6 3.8 %block.15 = (bf16[2,256,256]{2,1,0:T(8,128)(2,1)S(1)}, bf16[2,256,256]{2,1,0:T(8,128)(2,1)S(1)}, bf16[256,256]{1,0:T(8,128)(2,1)S(1)}, bf16[256,256]{1,0:T(8,128)(2,1)S(1)}) custom-call(u16[256,128]{1,0:T(8,128)(2,1)S(1)} %get-tuple-element.95.words_ref, bf16[512,1024]{1,0:T(8,128)(2,1)S(1)} %spread.2.refs_4_.refs_0_.refs_14_.refs_15_.refs_16_.refs_17_.refs_18_.refs_19_, ...), custom_call_target="tpu_custom_call" | custom-call | flops 5368709120 | bytes 65536 | tf_op jit(solution)/shard_map/block/pallas_call | solution.py:167
  71.4 5.3 %collective-permute-done.16.refs_6_ = bf16[2,256,256]{2,1,0:T(8,128)(2,1)S(1)} collective-permute-done((bf16[2,256,256]{2,1,0:T(8,128)(2,1)S(1)}, bf16[2,256,256]{2,1,0:T(8,128)(2,1)S(1)}, u32[]{:S(2)}, u32[]{:S(2)}) %collective-permute-start.16) | collective-permute-done | bytes 262176 | tf_op jit(solution)/shard_map/ppermute | solution.py:219
  76.6 0.0 collective-permute-start.24
  76.7 0.6 collective-permute-start.17
  77.2 1.2 %collective-permute-done.22.refs_12_ = bf16[2,256,256]{2,1,0:T(8,128)(2,1)S(1)} collective-permute-done((bf16[2,256,256]{2,1,0:T(8,128)(2,1)S(1)}, bf16[2,256,256]{2,1,0:T(8,128)(2,1)S(1)}, u32[]{:S(2)}, u32[]{:S(2)}) %collective-permute-start.22) | collective-permute-done | bytes 262176 | tf_op jit(solution)/shard_map/ppermute | solution.py:219
  78.5 0.0 collective-permute-start.13
  78.5 0.0 collective-permute-done.20.refs_10_
  78.5 0.6 collective-permute-start.11
  79.1 0.1 collective-permute-start.19
  79.2 2.3 %collective-permute-done.15.refs_4_.refs_5_ = bf16[2,256,256]{2,1,0:T(8,128)(2,1)S(1)} collective-permute-done((bf16[2,256,256]{2,1,0:T(8,128)(2,1)S(1)}, bf16[2,256,256]{2,1,0:T(8,128)(2,1)S(1)}, u32[]{:S(2)}, u32[]{:S(2)}) %collective-permute-start.15) | collective-permute-done | bytes 262176 | tf_op jit(solution)/shard_map/ppermute | solution.py:219
  81.4 0.0 collective-permute-start.23
  81.5 0.0 collective-permute-done.17.refs_7_
  81.5 0.5 collective-permute-start.21
  82.0 0.8 collective-permute-done.23.refs_13_
  82.8 0.2 collective-permute-done.21.refs_11_
  83.0 1.6 %fill.1 = bf16[512,2048]{1,0:T(8,128)(2,1)} custom-call(bf16[2,256,256]{2,1,0:T(8,128)(2,1)S(1)} %collective-permute-done.10.refs_18_.refs_0_, bf16[256,256]{1,0:T(8,128)(2,1)S(1)} %collective-permute-done.11.refs_1_, bf16[2,256,256]{2,1,0:T(8,128)(2,1)S(1)} %collective-permute-done.12.refs_18_.refs_2_, ...), custom_call_target="tpu_custom_call" | custom-call | tf_op jit(solution)/shard_map/fill/pallas_call | solution.py:200
  (15 shorter events, 0.1 us)
Async XLA Ops:
  0.0 8.0 %collective-permute-start.4 = (bf16[4096,256]{1,0:T(8,128)(2,1)}, bf16[4096,256]{1,0:T(8,128)(2,1)S(1)}, u32[]{:S(2)}, u32[]{:S(2)}) collective-permute-start(bf16[4096,256]{1,0:T(8,128)(2,1)} %bitcast.15), channel_id=1, source_target_pairs={{0,1},{1,0},{2,3},{3,2},{4,5},{5,4},{6,7},{7,6},{8,9},{9,8},{10,11... | collective-permute-start | bytes 6291464 | tf_op jit(solution)/shard_map/ppermute | solution.py:222
  1.4 13.6 %collective-permute-start = (u16[256,128]{1,0:T(8,128)(2,1)S(1)}, u16[256,128]{1,0:T(8,128)(2,1)S(1)}, u32[]{:S(2)}, u32[]{:S(2)}) collective-permute-start(u16[256,128]{1,0:T(8,128)(2,1)S(1)} %dynamic-slice_convert_fusion.refs_0_), channel_id=1, source_target_pairs={{0,4},{2,6},{4,0},{6,2},{8,12},{10,14},{12,8},{14,10},{1,5},{3,7},... | collective-permute-start | bytes 196616 | tf_op jit(solution)/shard_map/ppermute | solution.py:219
  4.0 10.9 %collective-permute-start.1 = (u16[256,128]{1,0:T(8,128)(2,1)S(1)}, u16[256,128]{1,0:T(8,128)(2,1)S(1)}, u32[]{:S(2)}, u32[]{:S(2)}) collective-permute-start(u16[256,128]{1,0:T(8,128)(2,1)S(1)} %dynamic-slice_convert_fusion.refs_0_), channel_id=1, source_target_pairs={{0,8},{2,10},{4,12},{6,14},{8,0},{10,2},{12,4},{14,6},{1,9},{3,11}... | collective-permute-start | bytes 196616 | tf_op jit(solution)/shard_map/ppermute | solution.py:219
  6.6 8.4 %collective-permute-start.2 = (u16[256,128]{1,0:T(8,128)(2,1)S(1)}, u16[256,128]{1,0:T(8,128)(2,1)S(1)}, u32[]{:S(2)}, u32[]{:S(2)}) collective-permute-start(u16[256,128]{1,0:T(8,128)(2,1)S(1)} %dynamic-slice_convert_fusion.refs_0_), channel_id=1, source_target_pairs={{0,12},{2,14},{4,8},{6,10},{8,4},{10,6},{12,0},{14,2},{1,13},{3,15... | collective-permute-start | bytes 196616 | tf_op jit(solution)/shard_map/ppermute | solution.py:219
  6.6 1.4 %collective-permute-start.3 = (s32[2048]{0:T(1024)}, s32[2048]{0:T(1024)S(1)}, u32[]{:S(2)}, u32[]{:S(2)}) collective-permute-start(s32[2048]{0:T(1024)} %param.4), channel_id=1, source_target_pairs={{0,1},{1,0},{2,3},{3,2},{4,5},{5,4},{6,7},{7,6},{8,9},{9,8},{10,11... | collective-permute-start | bytes 24584 | tf_op jit(solution)/shard_map/ppermute | solution.py:222
  8.0 1.6 %copy-start = (bf16[4096,1,256]{2,0,1:T(8,128)(2,1)S(1)}, bf16[4096,1,256]{2,0,1:T(8,128)(2,1)}, u32[]{:S(2)}) copy-start(bf16[4096,1,256]{2,0,1:T(8,128)(2,1)} %param.5) | copy-start | bytes 6291460
  9.6 0.7 copy-start.2
  14.9 3.5 %copy-start.1 = (bf16[4096,1,256]{2,0,1:T(8,128)(2,1)S(1)}, bf16[4096,1,256]{2,0,1:T(8,128)(2,1)}, u32[]{:S(2)}) copy-start(bf16[4096,1,256]{2,0,1:T(8,128)(2,1)} %param.5) | copy-start | bytes 6291460
  16.2 8.4 %collective-permute-start.5 = (u16[4,256,128]{2,1,0:T(8,128)(2,1)S(1)}, u16[4,256,128]{2,1,0:T(8,128)(2,1)S(1)}, u32[]{:S(2)}, u32[]{:S(2)}) collective-permute-start(u16[4,256,128]{2,1,0:T(8,128)(2,1)S(1)} %get-tuple-element.54.refs_0_), channel_id=1, source_target_pairs={{0,2},{2,0},{4,6},{6,4},{8,10},{10,8},{12,14},{14,12},{1,3},{3,1},... | collective-permute-start | bytes 786440 | tf_op jit(solution)/shard_map/ppermute | solution.py:219
  17.9 7.8 %collective-permute-start.8 = (u16[4,256,128]{2,1,0:T(8,128)(2,1)S(1)}, u16[4,256,128]{2,1,0:T(8,128)(2,1)S(1)}, u32[]{:S(2)}, u32[]{:S(2)}) collective-permute-start(u16[4,256,128]{2,1,0:T(8,128)(2,1)S(1)} %get-tuple-element.54.refs_0_), channel_id=1, source_target_pairs={{0,1},{1,0},{2,3},{3,2},{4,5},{5,4},{6,7},{7,6},{8,9},{9,8},{10,11... | collective-permute-start | bytes 786440 | tf_op jit(solution)/shard_map/ppermute | solution.py:222
  17.9 10.7 %collective-permute-start.6 = (bf16[512,1024]{1,0:T(8,128)(2,1)S(1)}, bf16[512,1024]{1,0:T(8,128)(2,1)S(1)}, u32[]{:S(2)}, u32[]{:S(2)}) collective-permute-start(bf16[512,1024]{1,0:T(8,128)(2,1)S(1)} %spread.2.refs_4_.refs_0_.refs_14_.refs_15_.refs_16_.refs_17_.refs_18_.refs_19_), channel_id=1, source_target_pairs={{0,1},{1,0},{2,3},{3,2},{4,5},{5,4},{6,7},{7,6},{8,9},{9,8},{10,11... | collective-permute-start | bytes 3145736 | tf_op jit(solution)/shard_map/ppermute | solution.py:222
  23.1 5.5 %collective-permute-start.7 = (bf16[512,1024]{1,0:T(8,128)(2,1)S(1)}, bf16[512,1024]{1,0:T(8,128)(2,1)S(1)}, u32[]{:S(2)}, u32[]{:S(2)}) collective-permute-start(bf16[512,1024]{1,0:T(8,128)(2,1)S(1)} %spread.3.refs_1_), channel_id=1, source_target_pairs={{0,1},{1,0},{2,3},{3,2},{4,5},{5,4},{6,7},{7,6},{8,9},{9,8},{10,11... | collective-permute-start | bytes 3145736 | tf_op jit(solution)/shard_map/ppermute | solution.py:222
  25.7 1.6 %collective-permute-start.9 = (u16[4,256,128]{2,1,0:T(8,128)(2,1)S(1)}, u16[4,256,128]{2,1,0:T(8,128)(2,1)S(1)}, u32[]{:S(2)}, u32[]{:S(2)}) collective-permute-start(u16[4,256,128]{2,1,0:T(8,128)(2,1)S(1)} %collective-permute-done.5.refs_0_), channel_id=1, source_target_pairs={{0,1},{1,0},{2,3},{3,2},{4,5},{5,4},{6,7},{7,6},{8,9},{9,8},{10,11... | collective-permute-start | bytes 786440 | tf_op jit(solution)/shard_map/ppermute | solution.py:222
  32.4 25.7 %collective-permute-start.10 = (bf16[2,256,256]{2,1,0:T(8,128)(2,1)S(1)}, bf16[2,256,256]{2,1,0:T(8,128)(2,1)S(1)}, u32[]{:S(2)}, u32[]{:S(2)}) collective-permute-start(bf16[2,256,256]{2,1,0:T(8,128)(2,1)S(1)} %get-tuple-element.64.refs_15_), channel_id=1, source_target_pairs={{0,14},{2,12},{4,10},{6,8},{8,6},{10,4},{12,2},{14,0},{1,15},{3,13... | collective-permute-start | bytes 786440 | tf_op jit(solution)/shard_map/ppermute | solution.py:219
  41.0 22.2 %collective-permute-start.12 = (bf16[2,256,256]{2,1,0:T(8,128)(2,1)S(1)}, bf16[2,256,256]{2,1,0:T(8,128)(2,1)S(1)}, u32[]{:S(2)}, u32[]{:S(2)}) collective-permute-start(bf16[2,256,256]{2,1,0:T(8,128)(2,1)S(1)} %get-tuple-element.69.refs_15_), channel_id=1, source_target_pairs={{0,12},{2,14},{4,8},{6,10},{8,4},{10,6},{12,0},{14,2},{1,13},{3,15... | collective-permute-start | bytes 786440 | tf_op jit(solution)/shard_map/ppermute | solution.py:219
  45.0 4.2 %collective-permute-start.14 = (bf16[256,256]{1,0:T(8,128)(2,1)S(1)}, bf16[256,256]{1,0:T(8,128)(2,1)S(1)}, u32[]{:S(2)}, u32[]{:S(2)}) collective-permute-start(bf16[256,256]{1,0:T(8,128)(2,1)S(1)} %get-tuple-element.76.refs_13_.refs_17_), channel_id=1, source_target_pairs={{0,1},{1,0},{2,3},{3,2},{4,5},{5,4},{6,7},{7,6},{8,9},{9,8},{10,11... | collective-permute-start | bytes 393224 | tf_op jit(solution)/shard_map/ppermute | solution.py:222
  49.1 27.5 %collective-permute-start.16 = (bf16[2,256,256]{2,1,0:T(8,128)(2,1)S(1)}, bf16[2,256,256]{2,1,0:T(8,128)(2,1)S(1)}, u32[]{:S(2)}, u32[]{:S(2)}) collective-permute-start(bf16[2,256,256]{2,1,0:T(8,128)(2,1)S(1)} %get-tuple-element.81.refs_15_), channel_id=1, source_target_pairs={{0,10},{2,8},{4,14},{6,12},{8,2},{10,0},{12,6},{14,4},{1,11},{3,9}... | collective-permute-start | bytes 786440 | tf_op jit(solution)/shard_map/ppermute | solution.py:219
  53.0 23.7 %collective-permute-start.18 = (bf16[2,256,256]{2,1,0:T(8,128)(2,1)S(1)}, bf16[2,256,256]{2,1,0:T(8,128)(2,1)S(1)}, u32[]{:S(2)}, u32[]{:S(2)}) collective-permute-start(bf16[2,256,256]{2,1,0:T(8,128)(2,1)S(1)} %get-tuple-element.85.refs_15_), channel_id=1, source_target_pairs={{0,6},{2,4},{4,2},{6,0},{8,14},{10,12},{12,10},{14,8},{1,7},{3,5},... | collective-permute-start | bytes 786440 | tf_op jit(solution)/shard_map/ppermute | solution.py:219
  58.1 23.4 %collective-permute-start.15 = (bf16[2,256,256]{2,1,0:T(8,128)(2,1)S(1)}, bf16[2,256,256]{2,1,0:T(8,128)(2,1)S(1)}, u32[]{:S(2)}, u32[]{:S(2)}) collective-permute-start(bf16[2,256,256]{2,1,0:T(8,128)(2,1)S(1)} %get-tuple-element.84.refs_14_.refs_19_), channel_id=1, source_target_pairs={{0,8},{2,10},{4,12},{6,14},{8,0},{10,2},{12,4},{14,6},{1,9},{3,11}... | collective-permute-start | bytes 786440 | tf_op jit(solution)/shard_map/ppermute | solution.py:219
  61.9 16.6 %collective-permute-start.20 = (bf16[2,256,256]{2,1,0:T(8,128)(2,1)S(1)}, bf16[2,256,256]{2,1,0:T(8,128)(2,1)S(1)}, u32[]{:S(2)}, u32[]{:S(2)}) collective-permute-start(bf16[2,256,256]{2,1,0:T(8,128)(2,1)S(1)} %get-tuple-element.89.refs_15_), channel_id=1, source_target_pairs={{0,4},{2,6},{4,0},{6,2},{8,12},{10,14},{12,8},{14,10},{1,5},{3,7},... | collective-permute-start | bytes 786440 | tf_op jit(solution)/shard_map/ppermute | solution.py:219
  67.0 11.5 %collective-permute-start.22 = (bf16[2,256,256]{2,1,0:T(8,128)(2,1)S(1)}, bf16[2,256,256]{2,1,0:T(8,128)(2,1)S(1)}, u32[]{:S(2)}, u32[]{:S(2)}) collective-permute-start(bf16[2,256,256]{2,1,0:T(8,128)(2,1)S(1)} %get-tuple-element.94.refs_15_), channel_id=1, source_target_pairs={{0,2},{2,0},{4,6},{6,4},{8,10},{10,8},{12,14},{14,12},{1,3},{3,1},... | collective-permute-start | bytes 786440 | tf_op jit(solution)/shard_map/ppermute | solution.py:219
  76.6 2.5 %collective-permute-start.24 = (bf16[256,256]{1,0:T(8,128)(2,1)S(1)}, bf16[256,256]{1,0:T(8,128)(2,1)S(1)}, u32[]{:S(2)}, u32[]{:S(2)}) collective-permute-start(bf16[256,256]{1,0:T(8,128)(2,1)S(1)} %get-tuple-element.100), channel_id=1, source_target_pairs={{0,1},{1,0},{2,3},{3,2},{4,5},{5,4},{6,7},{7,6},{8,9},{9,8},{10,11... | collective-permute-start | bytes 393224 | tf_op jit(solution)/shard_map/ppermute | solution.py:222
  76.7 4.8 %collective-permute-start.17 = (bf16[256,256]{1,0:T(8,128)(2,1)S(1)}, bf16[256,256]{1,0:T(8,128)(2,1)S(1)}, u32[]{:S(2)}, u32[]{:S(2)}) collective-permute-start(bf16[256,256]{1,0:T(8,128)(2,1)S(1)} %slice_bitcast_fusion.3), channel_id=1, source_target_pairs={{0,1},{1,0},{2,3},{3,2},{4,5},{5,4},{6,7},{7,6},{8,9},{9,8},{10,11... | collective-permute-start | bytes 393224 | tf_op jit(solution)/shard_map/ppermute | solution.py:222
  78.5 3.5 %collective-permute-start.13 = (bf16[256,256]{1,0:T(8,128)(2,1)S(1)}, bf16[256,256]{1,0:T(8,128)(2,1)S(1)}, u32[]{:S(2)}, u32[]{:S(2)}) collective-permute-start(bf16[256,256]{1,0:T(8,128)(2,1)S(1)} %slice_bitcast_fusion.4), channel_id=1, source_target_pairs={{0,1},{1,0},{2,3},{3,2},{4,5},{5,4},{6,7},{7,6},{8,9},{9,8},{10,11... | collective-permute-start | bytes 393224 | tf_op jit(solution)/shard_map/ppermute | solution.py:222
  78.5 3.5 %collective-permute-start.11 = (bf16[256,256]{1,0:T(8,128)(2,1)S(1)}, bf16[256,256]{1,0:T(8,128)(2,1)S(1)}, u32[]{:S(2)}, u32[]{:S(2)}) collective-permute-start(bf16[256,256]{1,0:T(8,128)(2,1)S(1)} %slice_bitcast_fusion.5), channel_id=1, source_target_pairs={{0,1},{1,0},{2,3},{3,2},{4,5},{5,4},{6,7},{7,6},{8,9},{9,8},{10,11... | collective-permute-start | bytes 393224 | tf_op jit(solution)/shard_map/ppermute | solution.py:222
  79.1 2.9 %collective-permute-start.19 = (bf16[256,256]{1,0:T(8,128)(2,1)S(1)}, bf16[256,256]{1,0:T(8,128)(2,1)S(1)}, u32[]{:S(2)}, u32[]{:S(2)}) collective-permute-start(bf16[256,256]{1,0:T(8,128)(2,1)S(1)} %slice_bitcast_fusion.2), channel_id=1, source_target_pairs={{0,1},{1,0},{2,3},{3,2},{4,5},{5,4},{6,7},{7,6},{8,9},{9,8},{10,11... | collective-permute-start | bytes 393224 | tf_op jit(solution)/shard_map/ppermute | solution.py:222
  81.4 1.3 %collective-permute-start.23 = (bf16[256,256]{1,0:T(8,128)(2,1)S(1)}, bf16[256,256]{1,0:T(8,128)(2,1)S(1)}, u32[]{:S(2)}, u32[]{:S(2)}) collective-permute-start(bf16[256,256]{1,0:T(8,128)(2,1)S(1)} %slice_bitcast_fusion), channel_id=1, source_target_pairs={{0,1},{1,0},{2,3},{3,2},{4,5},{5,4},{6,7},{7,6},{8,9},{9,8},{10,11... | collective-permute-start | bytes 393224 | tf_op jit(solution)/shard_map/ppermute | solution.py:222
  81.5 1.5 %collective-permute-start.21 = (bf16[256,256]{1,0:T(8,128)(2,1)S(1)}, bf16[256,256]{1,0:T(8,128)(2,1)S(1)}, u32[]{:S(2)}, u32[]{:S(2)}) collective-permute-start(bf16[256,256]{1,0:T(8,128)(2,1)S(1)} %slice_bitcast_fusion.1), channel_id=1, source_target_pairs={{0,1},{1,0},{2,3},{3,2},{4,5},{5,4},{6,7},{7,6},{8,9},{9,8},{10,11... | collective-permute-start | bytes 393224 | tf_op jit(solution)/shard_map/ppermute | solution.py:222
where the time goes:
time: 84.8 us; the launch traced here: 84.6 us
  Pallas kernels  46 us (54%)
  starting transfers between devices  22.1 us (26%)
  waiting for transfers between devices  12.9 us (15%)
  local copies, waits for them, and re-layouts  2.37 us (3%)
  other arithmetic  0.91 us (1%)
    pallas_call x8, Pallas kernels, block(): pl.pallas_call(functools.partial(block_kernel, sums=len(sums), pairs=len(...  30.3 us
    ppermute x11, starting transfers between devices, across(): return lax.ppermute(x, 'hit', [(i, i ^ k) for i in range(devices)])  19.2 us
    ppermute x11, waiting for transfers between devices, across(): return lax.ppermute(x, 'hit', [(i, i ^ k) for i in range(devices)])  10.1 us
    pallas_call x2, Pallas kernels, spread(): pl.pallas_call(functools.partial(spread_kernel, steps=steps, hit_rows=hit...  9.29 us
    pallas_call x4, Pallas kernels, unpack(): pl.pallas_call(functools.partial(unpack_kernel, count=count, stack=stack,...  4.78 us
    ppermute x14, starting transfers between devices, over(): return lax.ppermute(x, 'lm', [(0, 1), (1, 0)])  2.88 us
    ppermute x14, waiting for transfers between devices, over(): return lax.ppermute(x, 'lm', [(0, 1), (1, 0)])  2.78 us
    unnamed x6, local copies, waits for them, and re-layouts  2.29 us
  transfers between devices with their start and end apart: 25, of which 8 were waited for; matrix products, arithmetic and copies ran while one was open for 1% of the time, Pallas kernels for 47%

commit v1 on v0

--- a/solution.py
+++ b/solution.py
@@ -25,7 +25,7 @@
         for at in range(count):
             more[at - count][...] = word_ref[at]
 
-    @pl.loop(0, count)
+    @pl.loop(0, count, unroll=2)
     def _(at):
         words = word_ref[at].astype(jnp.int32)
         rows, width = words.shape
@@ -187,13 +187,19 @@
     out_ref = refs[-1]
     side = lax.axis_index("lm")
     me = lax.axis_index("hit")
-    for i, k in enumerate(steps):
-        for at, which in ((0, side), (1, 1 - side)):
-            ref = refs[2 * i + at]
-            piece = ref[at] if len(ref.shape) == 3 else ref[...]
-            rows, cols = piece.shape
-            row = pl.ds(pl.multiple_of(which * rows, rows), rows)
-            out_ref[row, pl.ds(pl.multiple_of((me ^ k) * cols, cols), cols)] = piece
+    rows, cols = refs[1].shape[-2:]
+    band = rows // 4
+
+    @pl.loop(0, rows // band)
+    def _(step):
+        low = pl.multiple_of(step * band, band)
+        for i, k in enumerate(steps):
+            for at, which in ((0, side), (1, 1 - side)):
+                ref = refs[2 * i + at]
+                here = pl.ds(low, band)
+                piece = ref[at, here, :] if len(ref.shape) == 3 else ref[here, :]
+                row = pl.ds(pl.multiple_of(which * rows + low, band), band)
+                out_ref[row, pl.ds(pl.multiple_of((me ^ k) * cols, cols), cols)] = piece
 
 
 def fill(steps, pieces, shape, after):
@@ -235,8 +241,9 @@
     words_odd = across(words_even, 1)
     sums.append(spread(odd, *args, [words_even]))
     sums += [over(x) for x in sums]
-    pair_odd, list_odd = unpack(words_odd, single=True)
-    pairs = [pair_even, pair_odd, unpack(over(words_even))[0], unpack(over(words_odd))[0]]
+    pair_even_sib, _ = unpack(over(words_even))
+    pair_odd, list_odd = unpack(words_odd, pair_even_sib[1:], single=True)
+    pairs = [pair_even, pair_odd, pair_even_sib, unpack(over(words_odd))[0]]
     words = dict(zip(even + odd, [*list_even, *list_odd]))
 
     order = list(range(devices - 1, -1, -1))

time: 84.8 us -> 83.7 us (0.987)
  no operation moved by 1% of the time
where the time goes in v1:
time: 83.7 us; the launch traced here: 83.5 us
  Pallas kernels  45.5 us (54%)
  starting transfers between devices  22.2 us (27%)
  waiting for transfers between devices  12.2 us (15%)
  local copies, waits for them, and re-layouts  2.37 us (3%)
  other arithmetic  0.91 us (1%)
    pallas_call x8, Pallas kernels, block(): pl.pallas_call(functools.partial(block_kernel, sums=len(sums), pairs=len(...  30.3 us
    ppermute x11, starting transfers between devices, across(): return lax.ppermute(x, 'hit', [(i, i ^ k) for i in range(devices)])  19.2 us
    ppermute x11, waiting for transfers between devices, across(): return lax.ppermute(x, 'hit', [(i, i ^ k) for i in range(devices)])  9.31 us
    pallas_call x2, Pallas kernels, spread(): pl.pallas_call(functools.partial(spread_kernel, steps=steps, hit_rows=hit...  9.29 us
    pallas_call x4, Pallas kernels, unpack(): pl.pallas_call(functools.partial(unpack_kernel, count=count, stack=stack,...  4.26 us
    ppermute x14, starting transfers between devices, over(): return lax.ppermute(x, 'lm', [(0, 1), (1, 0)])  3.04 us
    ppermute x14, waiting for transfers between devices, over(): return lax.ppermute(x, 'lm', [(0, 1), (1, 0)])  2.91 us
    unnamed x6, local copies, waits for them, and re-layouts  2.29 us
  transfers between devices with their start and end apart: 25, of which 8 were waited for; matrix products, arithmetic and copies ran while one was open for 1% of the time, Pallas kernels for 47%

profile of v1, /device:TPU:0, one launch (start us, length us, event | category | flops | bytes accessed | tf_op | source)
XLA Modules:
  0.0 83.5 jit_solution(11046258393691763416)
XLA Ops:
  0.0 0.5 collective-permute-start.4
  0.5 0.9 %dynamic-slice_convert_fusion.refs_0_ = u16[256,128]{1,0:T(8,128)(2,1)S(1)} fusion(s32[512,128]{1,0:T(8,128)} %param.3, s32[]{:T(128)S(6)} %select_n.3), kind=kLoop, calls=%fused_computation.6 | loop fusion | flops 32768 | bytes 196612 | tf_op jit(solution)/shard_map/convert_element_type | solution.py:230
  1.4 2.6 %collective-permute-start = (u16[256,128]{1,0:T(8,128)(2,1)S(1)}, u16[256,128]{1,0:T(8,128)(2,1)S(1)}, u32[]{:S(2)}, u32[]{:S(2)}) collective-permute-start(u16[256,128]{1,0:T(8,128)(2,1)S(1)} %dynamic-slice_convert_fusion.refs_0_), channel_id=1, source_target_pairs={{0,4},{2,6},{4,0},{6,2},{8,12},{10,14},{12,8},{14,10},{1,5},{3,7},... | collective-permute-start | bytes 196616 | tf_op jit(solution)/shard_map/ppermute | solution.py:225
  4.0 2.6 %collective-permute-start.1 = (u16[256,128]{1,0:T(8,128)(2,1)S(1)}, u16[256,128]{1,0:T(8,128)(2,1)S(1)}, u32[]{:S(2)}, u32[]{:S(2)}) collective-permute-start(u16[256,128]{1,0:T(8,128)(2,1)S(1)} %dynamic-slice_convert_fusion.refs_0_), channel_id=1, source_target_pairs={{0,8},{2,10},{4,12},{6,14},{8,0},{10,2},{12,4},{14,6},{1,9},{3,11}... | collective-permute-start | bytes 196616 | tf_op jit(solution)/shard_map/ppermute | solution.py:225
  6.6 0.0 collective-permute-start.2
  6.6 0.0 collective-permute-start.3
  6.6 1.4 %collective-permute-done.3 = s32[2048]{0:T(1024)S(1)} collective-permute-done((s32[2048]{0:T(1024)}, s32[2048]{0:T(1024)S(1)}, u32[]{:S(2)}, u32[]{:S(2)}) %collective-permute-start.3) | collective-permute-done | bytes 8224 | tf_op jit(solution)/shard_map/ppermute | solution.py:228
  8.0 0.0 collective-permute-done.4.sib_ref
  8.0 1.6 %copy-done = bf16[4096,1,256]{2,0,1:T(8,128)(2,1)S(1)} copy-done((bf16[4096,1,256]{2,0,1:T(8,128)(2,1)S(1)}, bf16[4096,1,256]{2,0,1:T(8,128)(2,1)}, u32[]{:S(2)}) %copy-start) | copy-done | bytes 2097176
  9.6 0.7 copy-done.2
  10.3 4.6 %spread.2.refs_4_.refs_0_.refs_14_.refs_15_.refs_16_.refs_17_.refs_18_.refs_19_ = bf16[512,1024]{1,0:T(8,128)(2,1)S(1)} custom-call(s32[1,2048]{1,0:T(1,128)S(1)} %bitcast.18, bf16[4096,256]{1,0:T(8,128)(2,1)S(1)} %bitcast.16, s32[1,2048]{1,0:T(1,128)S(1)} %bitcast.20, bf16[4096,256]{1,0:T(8,128)(2,1)S(1)} %collective-permute-done.4.sib_ref), custom_call_target="tpu_custom_call" | custom-call | flops 134217728 | bytes 1048576 | tf_op jit(solution)/shard_map/spread/pallas_call | solution.py:105
  14.9 0.0 copy-start.1
  14.9 0.0 collective-permute-done.refs_1_
  15.0 0.0 collective-permute-done.2.refs_3_
  15.0 1.1 %unpack.4 = (f8e4m3fn[1024,2048]{1,0:T(32,128)(4,1)S(1)}, f32[1024,128]{1,0:T(8,128)S(1)}, u16[4,256,128]{2,1,0:T(8,128)(2,1)S(1)}, u16[256,128]{1,0:T(8,128)(2,...) custom-call(u16[256,128]{1,0:T(8,128)(2,1)S(1)} %dynamic-slice_convert_fusion.refs_0_,, ...), custom_call_target="tpu_custom_call" | custom-call | flops 8589934592 | bytes 32768 | tf_op jit(solution)/shard_map/unpack/pallas_call | solution.py:52
  16.0 0.2 collective-permute-start.6
  16.2 1.7 %collective-permute-start.5 = (u16[4,256,128]{2,1,0:T(8,128)(2,1)S(1)}, u16[4,256,128]{2,1,0:T(8,128)(2,1)S(1)}, u32[]{:S(2)}, u32[]{:S(2)}) collective-permute-start(u16[4,256,128]{2,1,0:T(8,128)(2,1)S(1)} %get-tuple-element.54.refs_0_), channel_id=1, source_target_pairs={{0,2},{2,0},{4,6},{6,4},{8,10},{10,8},{12,14},{14,12},{1,3},{3,1},... | collective-permute-start | bytes 786440 | tf_op jit(solution)/shard_map/ppermute | solution.py:225
  18.0 0.1 collective-permute-start.7
  18.1 4.6 %spread.3.refs_1_ = bf16[512,1024]{1,0:T(8,128)(2,1)S(1)} custom-call(s32[1,2048]{1,0:T(1,128)S(1)} %bitcast.19, bf16[4096,256]{1,0:T(8,128)(2,1)S(1)} %bitcast.17, s32[1,2048]{1,0:T(1,128)S(1)} %bitcast.21, bf16[4096,256]{1,0:T(8,128)(2,1)S(1)} %collective-permute-done.4.sib_ref, u16[4,256,128]{2,1,0:T(8,128)(2,1)S(1)} %get-tuple-element.54.refs_0_), custom_call_target="tpu_custom_call" | custom-call | flops 134217728 | bytes 1048576 | tf_op jit(solution)/shard_map/spread/pallas_call | solution.py:105
  22.7 0.5 collective-permute-start.8
  23.2 0.0 collective-permute-done.6.refs_0_
  23.2 1.0 %unpack.5 = (f8e4m3fn[1024,2048]{1,0:T(32,128)(4,1)S(1)}, f32[1024,128]{1,0:T(8,128)S(1)}) custom-call(u16[4,256,128]{2,1,0:T(8,128)(2,1)S(1)} %collective-permute-done.6.refs_0_), custom_call_target="tpu_custom_call" | custom-call | flops 8589934592 | bytes 32768 | tf_op jit(solution)/shard_map/unpack/pallas_call | solution.py:52
  24.2 0.5 collective-permute-done.5.refs_0_
  24.8 0.0 collective-permute-start.9
  24.8 1.0 %unpack.6 = (f8e4m3fn[1024,2048]{1,0:T(32,128)(4,1)S(1)}, f32[1024,128]{1,0:T(8,128)S(1)}, u16[256,128]{1,0:T(8,128)(2,1)S(1)}, u16[256,128]{1,0:T(8,128)(2,1)S(...) custom-call(u16[4,256,128]{2,1,0:T(8,128)(2,1)S(1)} %collective-permute-done.5.refs_0_, ...), custom_call_target="tpu_custom_call" | custom-call | flops 8589934592 | bytes 32768 | tf_op jit(solution)/shard_map/unpack/pallas_call | solution.py:52
  25.8 0.5 collective-permute-done.9.refs_0_
  26.3 1.1 %unpack.7 = (f8e4m3fn[1024,2048]{1,0:T(32,128)(4,1)S(1)}, f32[1024,128]{1,0:T(8,128)S(1)}) custom-call(u16[4,256,128]{2,1,0:T(8,128)(2,1)S(1)} %collective-permute-done.9.refs_0_), custom_call_target="tpu_custom_call" | custom-call | flops 8589934592 | bytes 32768 | tf_op jit(solution)/shard_map/unpack/pallas_call | solution.py:52
  27.5 0.0 collective-permute-done.8.refs_3_
  27.5 0.0 collective-permute-done.7.refs_2_
  27.5 3.8 %block.8 = (bf16[2,256,256]{2,1,0:T(8,128)(2,1)S(1)}, bf16[2,256,256]{2,1,0:T(8,128)(2,1)S(1)}, bf16[256,256]{1,0:T(8,128)(2,1)S(1)}, bf16[256,256]{1,0:T(8,128)(2,1)S(1)}) custom-call(u16[256,128]{1,0:T(8,128)(2,1)S(1)} %get-tuple-element.56.words_ref, bf16[512,1024]{1,0:T(8,128)(2,1)S(1)} %spread.2.refs_4_.refs_0_.refs_14_.refs_15_.refs_16_.refs_17_.refs_18_.refs_19_, ...), custom_call_target="tpu_custom_call" | custom-call | flops 5368709120 | bytes 65536 | tf_op jit(solution)/shard_map/block/pallas_call | solution.py:167
  31.3 4.8 %collective-permute-start.10 = (bf16[2,256,256]{2,1,0:T(8,128)(2,1)S(1)}, bf16[2,256,256]{2,1,0:T(8,128)(2,1)S(1)}, u32[]{:S(2)}, u32[]{:S(2)}) collective-permute-start(bf16[2,256,256]{2,1,0:T(8,128)(2,1)S(1)} %get-tuple-element.64.refs_15_), channel_id=1, source_target_pairs={{0,14},{2,12},{4,10},{6,8},{8,6},{10,4},{12,2},{14,0},{1,15},{3,13... | collective-permute-start | bytes 786440 | tf_op jit(solution)/shard_map/ppermute | solution.py:225
  36.1 3.8 %block.9 = (bf16[2,256,256]{2,1,0:T(8,128)(2,1)S(1)}, bf16[2,256,256]{2,1,0:T(8,128)(2,1)S(1)}, bf16[256,256]{1,0:T(8,128)(2,1)S(1)}, bf16[256,256]{1,0:T(8,128)(2,1)S(1)}) custom-call(u16[256,128]{1,0:T(8,128)(2,1)S(1)} %get-tuple-element.65.words_ref, bf16[512,1024]{1,0:T(8,128)(2,1)S(1)} %spread.2.refs_4_.refs_0_.refs_14_.refs_15_.refs_16_.refs_17_.refs_18_.refs_19_, ...), custom_call_target="tpu_custom_call" | custom-call | flops 5368709120 | bytes 65536 | tf_op jit(solution)/shard_map/block/pallas_call | solution.py:167
  39.9 0.3 collective-permute-start.12
  40.2 3.8 %block.10 = (bf16[2,256,256]{2,1,0:T(8,128)(2,1)S(1)}, bf16[2,256,256]{2,1,0:T(8,128)(2,1)S(1)}, bf16[256,256]{1,0:T(8,128)(2,1)S(1)}, bf16[256,256]{1,0:T(8,128)(2,1)S(1)}) custom-call(u16[256,128]{1,0:T(8,128)(2,1)S(1)} %get-tuple-element.71.words_ref, bf16[512,1024]{1,0:T(8,128)(2,1)S(1)} %spread.2.refs_4_.refs_0_.refs_14_.refs_15_.refs_16_.refs_17_.refs_18_.refs_19_, ...), custom_call_target="tpu_custom_call" | custom-call | flops 5368709120 | bytes 65536 | tf_op jit(solution)/shard_map/block/pallas_call | solution.py:167
  43.9 0.1 collective-permute-start.14
  44.0 4.0 %block.11 = (bf16[2,256,256]{2,1,0:T(8,128)(2,1)S(1)}, bf16[2,256,256]{2,1,0:T(8,128)(2,1)S(1)}, bf16[256,256]{1,0:T(8,128)(2,1)S(1)}, bf16[256,256]{1,0:T(8,128)(2,1)S(1)}) custom-call(u16[256,128]{1,0:T(8,128)(2,1)S(1)} %get-tuple-element.77.words_ref, bf16[512,1024]{1,0:T(8,128)(2,1)S(1)} %spread.2.refs_4_.refs_0_.refs_14_.refs_15_.refs_16_.refs_17_.refs_18_.refs_19_, ...), custom_call_target="tpu_custom_call" | custom-call | flops 5368709120 | bytes 65536 | tf_op jit(solution)/shard_map/block/pallas_call | solution.py:167
  48.0 0.1 collective-permute-start.16
  48.1 0.0 collective-permute-done.14.refs_13_
  48.1 3.8 %block.12 = (bf16[2,256,256]{2,1,0:T(8,128)(2,1)S(1)}, bf16[2,256,256]{2,1,0:T(8,128)(2,1)S(1)}, bf16[256,256]{1,0:T(8,128)(2,1)S(1)}, bf16[256,256]{1,0:T(8,128)(2,1)S(1)}) custom-call(u16[256,128]{1,0:T(8,128)(2,1)S(1)} %get-tuple-element.70.words_ref, bf16[512,1024]{1,0:T(8,128)(2,1)S(1)} %spread.2.refs_4_.refs_0_.refs_14_.refs_15_.refs_16_.refs_17_.refs_18_.refs_19_, ...), custom_call_target="tpu_custom_call" | custom-call | flops 5368709120 | bytes 65536 | tf_op jit(solution)/shard_map/block/pallas_call | solution.py:167
  51.9 5.1 %collective-permute-start.18 = (bf16[2,256,256]{2,1,0:T(8,128)(2,1)S(1)}, bf16[2,256,256]{2,1,0:T(8,128)(2,1)S(1)}, u32[]{:S(2)}, u32[]{:S(2)}) collective-permute-start(bf16[2,256,256]{2,1,0:T(8,128)(2,1)S(1)} %get-tuple-element.85.refs_15_), channel_id=1, source_target_pairs={{0,6},{2,4},{4,2},{6,0},{8,14},{10,12},{12,10},{14,8},{1,7},{3,5},... | collective-permute-start | bytes 786440 | tf_op jit(solution)/shard_map/ppermute | solution.py:225
  57.0 0.0 collective-permute-start.15
  57.0 0.0 collective-permute-done.10.refs_18_.refs_0_
  57.0 3.8 %block.13 = (bf16[2,256,256]{2,1,0:T(8,128)(2,1)S(1)}, bf16[2,256,256]{2,1,0:T(8,128)(2,1)S(1)}, bf16[256,256]{1,0:T(8,128)(2,1)S(1)}, bf16[256,256]{1,0:T(8,128)(2,1)S(1)}) custom-call(u16[256,128]{1,0:T(8,128)(2,1)S(1)} %get-tuple-element.86.words_ref, bf16[512,1024]{1,0:T(8,128)(2,1)S(1)} %spread.2.refs_4_.refs_0_.refs_14_.refs_15_.refs_16_.refs_17_.refs_18_.refs_19_, ...), custom_call_target="tpu_custom_call" | custom-call | flops 5368709120 | bytes 65536 | tf_op jit(solution)/shard_map/block/pallas_call | solution.py:167
  60.8 1.4 %collective-permute-start.20 = (bf16[2,256,256]{2,1,0:T(8,128)(2,1)S(1)}, bf16[2,256,256]{2,1,0:T(8,128)(2,1)S(1)}, u32[]{:S(2)}, u32[]{:S(2)}) collective-permute-start(bf16[2,256,256]{2,1,0:T(8,128)(2,1)S(1)} %get-tuple-element.89.refs_15_), channel_id=1, source_target_pairs={{0,4},{2,6},{4,0},{6,2},{8,12},{10,14},{12,8},{14,10},{1,5},{3,7},... | collective-permute-start | bytes 786440 | tf_op jit(solution)/shard_map/ppermute | solution.py:225
  62.1 0.0 collective-permute-done.12.refs_18_.refs_2_
  62.1 3.8 %block.14 = (bf16[2,256,256]{2,1,0:T(8,128)(2,1)S(1)}, bf16[2,256,256]{2,1,0:T(8,128)(2,1)S(1)}, bf16[256,256]{1,0:T(8,128)(2,1)S(1)}, bf16[256,256]{1,0:T(8,128)(2,1)S(1)}) custom-call(u16[256,128]{1,0:T(8,128)(2,1)S(1)} %get-tuple-element.90.words_ref, bf16[512,1024]{1,0:T(8,128)(2,1)S(1)} %spread.2.refs_4_.refs_0_.refs_14_.refs_15_.refs_16_.refs_17_.refs_18_.refs_19_, ...), custom_call_target="tpu_custom_call" | custom-call | flops 5368709120 | bytes 65536 | tf_op jit(solution)/shard_map/block/pallas_call | solution.py:167
  65.9 0.6 collective-permute-start.22
  66.5 3.8 %block.15 = (bf16[2,256,256]{2,1,0:T(8,128)(2,1)S(1)}, bf16[2,256,256]{2,1,0:T(8,128)(2,1)S(1)}, bf16[256,256]{1,0:T(8,128)(2,1)S(1)}, bf16[256,256]{1,0:T(8,128)(2,1)S(1)}) custom-call(u16[256,128]{1,0:T(8,128)(2,1)S(1)} %get-tuple-element.95.words_ref, bf16[512,1024]{1,0:T(8,128)(2,1)S(1)} %spread.2.refs_4_.refs_0_.refs_14_.refs_15_.refs_16_.refs_17_.refs_18_.refs_19_, ...), custom_call_target="tpu_custom_call" | custom-call | flops 5368709120 | bytes 65536 | tf_op jit(solution)/shard_map/block/pallas_call | solution.py:167
  70.3 5.3 %collective-permute-done.16.refs_6_ = bf16[2,256,256]{2,1,0:T(8,128)(2,1)S(1)} collective-permute-done((bf16[2,256,256]{2,1,0:T(8,128)(2,1)S(1)}, bf16[2,256,256]{2,1,0:T(8,128)(2,1)S(1)}, u32[]{:S(2)}, u32[]{:S(2)}) %collective-permute-start.16) | collective-permute-done | bytes 262176 | tf_op jit(solution)/shard_map/ppermute | solution.py:225
  75.6 0.6 collective-permute-start.17
  76.1 1.2 %collective-permute-done.22.refs_12_ = bf16[2,256,256]{2,1,0:T(8,128)(2,1)S(1)} collective-permute-done((bf16[2,256,256]{2,1,0:T(8,128)(2,1)S(1)}, bf16[2,256,256]{2,1,0:T(8,128)(2,1)S(1)}, u32[]{:S(2)}, u32[]{:S(2)}) %collective-permute-start.22) | collective-permute-done | bytes 262176 | tf_op jit(solution)/shard_map/ppermute | solution.py:225
  77.4 0.0 collective-permute-start.13
  77.4 0.0 collective-permute-done.20.refs_10_
  77.4 0.6 collective-permute-start.11
  78.0 0.1 collective-permute-start.19
  78.1 2.3 %collective-permute-done.15.refs_4_.refs_5_ = bf16[2,256,256]{2,1,0:T(8,128)(2,1)S(1)} collective-permute-done((bf16[2,256,256]{2,1,0:T(8,128)(2,1)S(1)}, bf16[2,256,256]{2,1,0:T(8,128)(2,1)S(1)}, u32[]{:S(2)}, u32[]{:S(2)}) %collective-permute-start.15) | collective-permute-done | bytes 262176 | tf_op jit(solution)/shard_map/ppermute | solution.py:225
  80.3 0.0 collective-permute-start.23
  80.3 0.0 collective-permute-done.17.refs_7_
  80.4 0.5 collective-permute-start.21
  80.9 0.0 collective-permute-done.13.refs_3_
  80.9 0.0 collective-permute-done.11.refs_1_
  80.9 0.8 collective-permute-done.23.refs_13_
  81.7 0.2 collective-permute-done.21.refs_11_
  81.9 1.6 %fill.1 = bf16[512,2048]{1,0:T(8,128)(2,1)} custom-call(bf16[2,256,256]{2,1,0:T(8,128)(2,1)S(1)} %collective-permute-done.10.refs_18_.refs_0_, bf16[256,256]{1,0:T(8,128)(2,1)S(1)} %collective-permute-done.11.refs_1_, bf16[2,256,256]{2,1,0:T(8,128)(2,1)S(1)} %collective-permute-done.12.refs_18_.refs_2_, ...), custom_call_target="tpu_custom_call" | custom-call | tf_op jit(solution)/shard_map/fill/pallas_call | solution.py:206
  (15 shorter events, 0.1 us)
Async XLA Ops:
  0.0 8.0 %collective-permute-start.4 = (bf16[4096,256]{1,0:T(8,128)(2,1)}, bf16[4096,256]{1,0:T(8,128)(2,1)S(1)}, u32[]{:S(2)}, u32[]{:S(2)}) collective-permute-start(bf16[4096,256]{1,0:T(8,128)(2,1)} %bitcast.15), channel_id=1, source_target_pairs={{0,1},{1,0},{2,3},{3,2},{4,5},{5,4},{6,7},{7,6},{8,9},{9,8},{10,11... | collective-permute-start | bytes 6291464 | tf_op jit(solution)/shard_map/ppermute | solution.py:228
  1.4 13.6 %collective-permute-start = (u16[256,128]{1,0:T(8,128)(2,1)S(1)}, u16[256,128]{1,0:T(8,128)(2,1)S(1)}, u32[]{:S(2)}, u32[]{:S(2)}) collective-permute-start(u16[256,128]{1,0:T(8,128)(2,1)S(1)} %dynamic-slice_convert_fusion.refs_0_), channel_id=1, source_target_pairs={{0,4},{2,6},{4,0},{6,2},{8,12},{10,14},{12,8},{14,10},{1,5},{3,7},... | collective-permute-start | bytes 196616 | tf_op jit(solution)/shard_map/ppermute | solution.py:225
  4.0 10.9 %collective-permute-start.1 = (u16[256,128]{1,0:T(8,128)(2,1)S(1)}, u16[256,128]{1,0:T(8,128)(2,1)S(1)}, u32[]{:S(2)}, u32[]{:S(2)}) collective-permute-start(u16[256,128]{1,0:T(8,128)(2,1)S(1)} %dynamic-slice_convert_fusion.refs_0_), channel_id=1, source_target_pairs={{0,8},{2,10},{4,12},{6,14},{8,0},{10,2},{12,4},{14,6},{1,9},{3,11}... | collective-permute-start | bytes 196616 | tf_op jit(solution)/shard_map/ppermute | solution.py:225
  6.6 8.4 %collective-permute-start.2 = (u16[256,128]{1,0:T(8,128)(2,1)S(1)}, u16[256,128]{1,0:T(8,128)(2,1)S(1)}, u32[]{:S(2)}, u32[]{:S(2)}) collective-permute-start(u16[256,128]{1,0:T(8,128)(2,1)S(1)} %dynamic-slice_convert_fusion.refs_0_), channel_id=1, source_target_pairs={{0,12},{2,14},{4,8},{6,10},{8,4},{10,6},{12,0},{14,2},{1,13},{3,15... | collective-permute-start | bytes 196616 | tf_op jit(solution)/shard_map/ppermute | solution.py:225
  6.6 1.4 %collective-permute-start.3 = (s32[2048]{0:T(1024)}, s32[2048]{0:T(1024)S(1)}, u32[]{:S(2)}, u32[]{:S(2)}) collective-permute-start(s32[2048]{0:T(1024)} %param.4), channel_id=1, source_target_pairs={{0,1},{1,0},{2,3},{3,2},{4,5},{5,4},{6,7},{7,6},{8,9},{9,8},{10,11... | collective-permute-start | bytes 24584 | tf_op jit(solution)/shard_map/ppermute | solution.py:228
  8.0 1.6 %copy-start = (bf16[4096,1,256]{2,0,1:T(8,128)(2,1)S(1)}, bf16[4096,1,256]{2,0,1:T(8,128)(2,1)}, u32[]{:S(2)}) copy-start(bf16[4096,1,256]{2,0,1:T(8,128)(2,1)} %param.5) | copy-start | bytes 6291460
  9.6 0.7 copy-start.2
  14.9 3.1 %copy-start.1 = (bf16[4096,1,256]{2,0,1:T(8,128)(2,1)S(1)}, bf16[4096,1,256]{2,0,1:T(8,128)(2,1)}, u32[]{:S(2)}) copy-start(bf16[4096,1,256]{2,0,1:T(8,128)(2,1)} %param.5) | copy-start | bytes 6291460
  16.0 7.2 %collective-permute-start.6 = (u16[4,256,128]{2,1,0:T(8,128)(2,1)S(1)}, u16[4,256,128]{2,1,0:T(8,128)(2,1)S(1)}, u32[]{:S(2)}, u32[]{:S(2)}) collective-permute-start(u16[4,256,128]{2,1,0:T(8,128)(2,1)S(1)} %get-tuple-element.54.refs_0_), channel_id=1, source_target_pairs={{0,1},{1,0},{2,3},{3,2},{4,5},{5,4},{6,7},{7,6},{8,9},{9,8},{10,11... | collective-permute-start | bytes 786440 | tf_op jit(solution)/shard_map/ppermute | solution.py:228
  16.2 8.6 %collective-permute-start.5 = (u16[4,256,128]{2,1,0:T(8,128)(2,1)S(1)}, u16[4,256,128]{2,1,0:T(8,128)(2,1)S(1)}, u32[]{:S(2)}, u32[]{:S(2)}) collective-permute-start(u16[4,256,128]{2,1,0:T(8,128)(2,1)S(1)} %get-tuple-element.54.refs_0_), channel_id=1, source_target_pairs={{0,2},{2,0},{4,6},{6,4},{8,10},{10,8},{12,14},{14,12},{1,3},{3,1},... | collective-permute-start | bytes 786440 | tf_op jit(solution)/shard_map/ppermute | solution.py:225
  18.0 9.5 %collective-permute-start.7 = (bf16[512,1024]{1,0:T(8,128)(2,1)S(1)}, bf16[512,1024]{1,0:T(8,128)(2,1)S(1)}, u32[]{:S(2)}, u32[]{:S(2)}) collective-permute-start(bf16[512,1024]{1,0:T(8,128)(2,1)S(1)} %spread.2.refs_4_.refs_0_.refs_14_.refs_15_.refs_16_.refs_17_.refs_18_.refs_19_), channel_id=1, source_target_pairs={{0,1},{1,0},{2,3},{3,2},{4,5},{5,4},{6,7},{7,6},{8,9},{9,8},{10,11... | collective-permute-start | bytes 3145736 | tf_op jit(solution)/shard_map/ppermute | solution.py:228
  22.7 4.8 %collective-permute-start.8 = (bf16[512,1024]{1,0:T(8,128)(2,1)S(1)}, bf16[512,1024]{1,0:T(8,128)(2,1)S(1)}, u32[]{:S(2)}, u32[]{:S(2)}) collective-permute-start(bf16[512,1024]{1,0:T(8,128)(2,1)S(1)} %spread.3.refs_1_), channel_id=1, source_target_pairs={{0,1},{1,0},{2,3},{3,2},{4,5},{5,4},{6,7},{7,6},{8,9},{9,8},{10,11... | collective-permute-start | bytes 3145736 | tf_op jit(solution)/shard_map/ppermute | solution.py:228
  24.8 1.5 %collective-permute-start.9 = (u16[4,256,128]{2,1,0:T(8,128)(2,1)S(1)}, u16[4,256,128]{2,1,0:T(8,128)(2,1)S(1)}, u32[]{:S(2)}, u32[]{:S(2)}) collective-permute-start(u16[4,256,128]{2,1,0:T(8,128)(2,1)S(1)} %collective-permute-done.5.refs_0_), channel_id=1, source_target_pairs={{0,1},{1,0},{2,3},{3,2},{4,5},{5,4},{6,7},{7,6},{8,9},{9,8},{10,11... | collective-permute-start | bytes 786440 | tf_op jit(solution)/shard_map/ppermute | solution.py:228
  31.3 25.7 %collective-permute-start.10 = (bf16[2,256,256]{2,1,0:T(8,128)(2,1)S(1)}, bf16[2,256,256]{2,1,0:T(8,128)(2,1)S(1)}, u32[]{:S(2)}, u32[]{:S(2)}) collective-permute-start(bf16[2,256,256]{2,1,0:T(8,128)(2,1)S(1)} %get-tuple-element.64.refs_15_), channel_id=1, source_target_pairs={{0,14},{2,12},{4,10},{6,8},{8,6},{10,4},{12,2},{14,0},{1,15},{3,13... | collective-permute-start | bytes 786440 | tf_op jit(solution)/shard_map/ppermute | solution.py:225
  39.9 22.2 %collective-permute-start.12 = (bf16[2,256,256]{2,1,0:T(8,128)(2,1)S(1)}, bf16[2,256,256]{2,1,0:T(8,128)(2,1)S(1)}, u32[]{:S(2)}, u32[]{:S(2)}) collective-permute-start(bf16[2,256,256]{2,1,0:T(8,128)(2,1)S(1)} %get-tuple-element.69.refs_15_), channel_id=1, source_target_pairs={{0,12},{2,14},{4,8},{6,10},{8,4},{10,6},{12,0},{14,2},{1,13},{3,15... | collective-permute-start | bytes 786440 | tf_op jit(solution)/shard_map/ppermute | solution.py:225
  43.9 4.2 %collective-permute-start.14 = (bf16[256,256]{1,0:T(8,128)(2,1)S(1)}, bf16[256,256]{1,0:T(8,128)(2,1)S(1)}, u32[]{:S(2)}, u32[]{:S(2)}) collective-permute-start(bf16[256,256]{1,0:T(8,128)(2,1)S(1)} %get-tuple-element.76.refs_13_.refs_17_), channel_id=1, source_target_pairs={{0,1},{1,0},{2,3},{3,2},{4,5},{5,4},{6,7},{7,6},{8,9},{9,8},{10,11... | collective-permute-start | bytes 393224 | tf_op jit(solution)/shard_map/ppermute | solution.py:228
  48.0 27.5 %collective-permute-start.16 = (bf16[2,256,256]{2,1,0:T(8,128)(2,1)S(1)}, bf16[2,256,256]{2,1,0:T(8,128)(2,1)S(1)}, u32[]{:S(2)}, u32[]{:S(2)}) collective-permute-start(bf16[2,256,256]{2,1,0:T(8,128)(2,1)S(1)} %get-tuple-element.81.refs_15_), channel_id=1, source_target_pairs={{0,10},{2,8},{4,14},{6,12},{8,2},{10,0},{12,6},{14,4},{1,11},{3,9}... | collective-permute-start | bytes 786440 | tf_op jit(solution)/shard_map/ppermute | solution.py:225
  51.9 23.7 %collective-permute-start.18 = (bf16[2,256,256]{2,1,0:T(8,128)(2,1)S(1)}, bf16[2,256,256]{2,1,0:T(8,128)(2,1)S(1)}, u32[]{:S(2)}, u32[]{:S(2)}) collective-permute-start(bf16[2,256,256]{2,1,0:T(8,128)(2,1)S(1)} %get-tuple-element.85.refs_15_), channel_id=1, source_target_pairs={{0,6},{2,4},{4,2},{6,0},{8,14},{10,12},{12,10},{14,8},{1,7},{3,5},... | collective-permute-start | bytes 786440 | tf_op jit(solution)/shard_map/ppermute | solution.py:225
  57.0 23.3 %collective-permute-start.15 = (bf16[2,256,256]{2,1,0:T(8,128)(2,1)S(1)}, bf16[2,256,256]{2,1,0:T(8,128)(2,1)S(1)}, u32[]{:S(2)}, u32[]{:S(2)}) collective-permute-start(bf16[2,256,256]{2,1,0:T(8,128)(2,1)S(1)} %get-tuple-element.84.refs_14_.refs_19_), channel_id=1, source_target_pairs={{0,8},{2,10},{4,12},{6,14},{8,0},{10,2},{12,4},{14,6},{1,9},{3,11}... | collective-permute-start | bytes 786440 | tf_op jit(solution)/shard_map/ppermute | solution.py:225
  60.8 16.6 %collective-permute-start.20 = (bf16[2,256,256]{2,1,0:T(8,128)(2,1)S(1)}, bf16[2,256,256]{2,1,0:T(8,128)(2,1)S(1)}, u32[]{:S(2)}, u32[]{:S(2)}) collective-permute-start(bf16[2,256,256]{2,1,0:T(8,128)(2,1)S(1)} %get-tuple-element.89.refs_15_), channel_id=1, source_target_pairs={{0,4},{2,6},{4,0},{6,2},{8,12},{10,14},{12,8},{14,10},{1,5},{3,7},... | collective-permute-start | bytes 786440 | tf_op jit(solution)/shard_map/ppermute | solution.py:225
  65.9 11.5 %collective-permute-start.22 = (bf16[2,256,256]{2,1,0:T(8,128)(2,1)S(1)}, bf16[2,256,256]{2,1,0:T(8,128)(2,1)S(1)}, u32[]{:S(2)}, u32[]{:S(2)}) collective-permute-start(bf16[2,256,256]{2,1,0:T(8,128)(2,1)S(1)} %get-tuple-element.94.refs_15_), channel_id=1, source_target_pairs={{0,2},{2,0},{4,6},{6,4},{8,10},{10,8},{12,14},{14,12},{1,3},{3,1},... | collective-permute-start | bytes 786440 | tf_op jit(solution)/shard_map/ppermute | solution.py:225
  75.5 2.5 %collective-permute-start.24 = (bf16[256,256]{1,0:T(8,128)(2,1)S(1)}, bf16[256,256]{1,0:T(8,128)(2,1)S(1)}, u32[]{:S(2)}, u32[]{:S(2)}) collective-permute-start(bf16[256,256]{1,0:T(8,128)(2,1)S(1)} %get-tuple-element.100), channel_id=1, source_target_pairs={{0,1},{1,0},{2,3},{3,2},{4,5},{5,4},{6,7},{7,6},{8,9},{9,8},{10,11... | collective-permute-start | bytes 393224 | tf_op jit(solution)/shard_map/ppermute | solution.py:228
  75.6 4.8 %collective-permute-start.17 = (bf16[256,256]{1,0:T(8,128)(2,1)S(1)}, bf16[256,256]{1,0:T(8,128)(2,1)S(1)}, u32[]{:S(2)}, u32[]{:S(2)}) collective-permute-start(bf16[256,256]{1,0:T(8,128)(2,1)S(1)} %slice_bitcast_fusion.3), channel_id=1, source_target_pairs={{0,1},{1,0},{2,3},{3,2},{4,5},{5,4},{6,7},{7,6},{8,9},{9,8},{10,11... | collective-permute-start | bytes 393224 | tf_op jit(solution)/shard_map/ppermute | solution.py:228
  77.4 3.5 %collective-permute-start.13 = (bf16[256,256]{1,0:T(8,128)(2,1)S(1)}, bf16[256,256]{1,0:T(8,128)(2,1)S(1)}, u32[]{:S(2)}, u32[]{:S(2)}) collective-permute-start(bf16[256,256]{1,0:T(8,128)(2,1)S(1)} %slice_bitcast_fusion.4), channel_id=1, source_target_pairs={{0,1},{1,0},{2,3},{3,2},{4,5},{5,4},{6,7},{7,6},{8,9},{9,8},{10,11... | collective-permute-start | bytes 393224 | tf_op jit(solution)/shard_map/ppermute | solution.py:228
  77.4 3.5 %collective-permute-start.11 = (bf16[256,256]{1,0:T(8,128)(2,1)S(1)}, bf16[256,256]{1,0:T(8,128)(2,1)S(1)}, u32[]{:S(2)}, u32[]{:S(2)}) collective-permute-start(bf16[256,256]{1,0:T(8,128)(2,1)S(1)} %slice_bitcast_fusion.5), channel_id=1, source_target_pairs={{0,1},{1,0},{2,3},{3,2},{4,5},{5,4},{6,7},{7,6},{8,9},{9,8},{10,11... | collective-permute-start | bytes 393224 | tf_op jit(solution)/shard_map/ppermute | solution.py:228
  78.0 2.9 %collective-permute-start.19 = (bf16[256,256]{1,0:T(8,128)(2,1)S(1)}, bf16[256,256]{1,0:T(8,128)(2,1)S(1)}, u32[]{:S(2)}, u32[]{:S(2)}) collective-permute-start(bf16[256,256]{1,0:T(8,128)(2,1)S(1)} %slice_bitcast_fusion.2), channel_id=1, source_target_pairs={{0,1},{1,0},{2,3},{3,2},{4,5},{5,4},{6,7},{7,6},{8,9},{9,8},{10,11... | collective-permute-start | bytes 393224 | tf_op jit(solution)/shard_map/ppermute | solution.py:228
  80.3 1.3 %collective-permute-start.23 = (bf16[256,256]{1,0:T(8,128)(2,1)S(1)}, bf16[256,256]{1,0:T(8,128)(2,1)S(1)}, u32[]{:S(2)}, u32[]{:S(2)}) collective-permute-start(bf16[256,256]{1,0:T(8,128)(2,1)S(1)} %slice_bitcast_fusion), channel_id=1, source_target_pairs={{0,1},{1,0},{2,3},{3,2},{4,5},{5,4},{6,7},{7,6},{8,9},{9,8},{10,11... | collective-permute-start | bytes 393224 | tf_op jit(solution)/shard_map/ppermute | solution.py:228
  80.4 1.5 %collective-permute-start.21 = (bf16[256,256]{1,0:T(8,128)(2,1)S(1)}, bf16[256,256]{1,0:T(8,128)(2,1)S(1)}, u32[]{:S(2)}, u32[]{:S(2)}) collective-permute-start(bf16[256,256]{1,0:T(8,128)(2,1)S(1)} %slice_bitcast_fusion.1), channel_id=1, source_target_pairs={{0,1},{1,0},{2,3},{3,2},{4,5},{5,4},{6,7},{7,6},{8,9},{9,8},{10,11... | collective-permute-start | bytes 393224 | tf_op jit(solution)/shard_map/ppermute | solution.py:228

commit v2 on v1

--- a/solution.py
+++ b/solution.py
@@ -67,6 +67,24 @@
         name="unpack",
     )(*words, *after)
     return tuple(out[:2]), out[2:]
+
+
+def fetch_kernel(in_ref, out_ref, sem):
+    copy = pltpu.make_async_copy(in_ref, out_ref, sem)
+    copy.start()
+    copy.wait()
+
+
+def fetch(x):
+    return pl.pallas_call(
+        fetch_kernel,
+        in_specs=[ANY],
+        out_specs=VMEM,
+        out_shape=jax.ShapeDtypeStruct(x.shape, x.dtype),
+        scratch_shapes=[pltpu.SemaphoreType.DMA],
+        compiler_params=pltpu.CompilerParams(vmem_limit_bytes=24 * 2**20),
+        name="fetch",
+    )(x)
 
 
 def spread_kernel(mine_ref, own_ref, other_ref, sib_ref, *refs, steps, hit_rows, chunk):
@@ -235,7 +253,7 @@
     odd = [k ^ 1 for k in even]
     words_z = [across(mine, k) if k else mine for k in even]
 
-    args = (hit_rows, pick_list.reshape(1, -1), weight, other_picks.reshape(1, -1), other_weight)
+    args = (hit_rows, pick_list.reshape(1, -1), fetch(weight), other_picks.reshape(1, -1), other_weight)
     sums = [spread(even, *args, [])]
     pair_even, (words_even, *list_even) = unpack(words_z, sums, True, True)
     words_odd = across(words_even, 1)

time: 83.7 us -> 81.8 us (0.977)
  waiting for transfers between devices: 12.2 us -> 10.6 us
    ppermute x14, waiting for transfers between devices: 2.91 us -> 1.53 us  [over(): return lax.ppermute(x, 'lm', [(0, 1), (1, 0)])]
    unnamed x6 -> x4, local copies, waits for them, and re-layouts: 2.29 us -> 1.59 us
  transfers between devices with their start and end apart: 25 -> 25, of which waited for: 8 -> 7; matrix products, arithmetic and copies ran while one was open for 1% -> 1% of each run, Pallas kernels for 47% -> 48%
where the time goes in v2:
time: 81.8 us; the launch traced here: 81.6 us
  Pallas kernels  45.6 us (56%)
  starting transfers between devices  22.6 us (28%)
  waiting for transfers between devices  10.6 us (13%)
  local copies, waits for them, and re-layouts  1.67 us (2%)
  other arithmetic  0.93 us (1%)
    pallas_call x8, Pallas kernels, block(): pl.pallas_call(functools.partial(block_kernel, sums=len(sums), pairs=len(...  30.3 us
    ppermute x11, starting transfers between devices, across(): return lax.ppermute(x, 'hit', [(i, i ^ k) for i in range(devices)])  19.2 us
    pallas_call x2, Pallas kernels, spread(): pl.pallas_call(functools.partial(spread_kernel, steps=steps, hit_rows=hit...  9.29 us
    ppermute x11, waiting for transfers between devices, across(): return lax.ppermute(x, 'hit', [(i, i ^ k) for i in range(devices)])  9.05 us
    pallas_call x4, Pallas kernels, unpack(): pl.pallas_call(functools.partial(unpack_kernel, count=count, stack=stack,...  4.26 us
    ppermute x14, starting transfers between devices, over(): return lax.ppermute(x, 'lm', [(0, 1), (1, 0)])  3.38 us
  transfers between devices with their start and end apart: 25, of which 7 were waited for; matrix products, arithmetic and copies ran while one was open for 1% of the time, Pallas kernels for 48%

profile of v2, /device:TPU:0, one launch (start us, length us, event | category | flops | bytes accessed | tf_op | source)
XLA Modules:
  0.0 81.6 jit_solution(13867964048590958158)
XLA Ops:
  0.0 0.5 collective-permute-start.4
  0.5 0.9 %dynamic-slice_convert_fusion.refs_0_ = u16[256,128]{1,0:T(8,128)(2,1)S(1)} fusion(s32[512,128]{1,0:T(8,128)} %param.3, s32[]{:T(128)S(6)} %select_n.3), kind=kLoop, calls=%fused_computation.6 | loop fusion | flops 32768 | bytes 196612 | tf_op jit(solution)/shard_map/convert_element_type | solution.py:248
  1.4 2.6 %collective-permute-start = (u16[256,128]{1,0:T(8,128)(2,1)S(1)}, u16[256,128]{1,0:T(8,128)(2,1)S(1)}, u32[]{:S(2)}, u32[]{:S(2)}) collective-permute-start(u16[256,128]{1,0:T(8,128)(2,1)S(1)} %dynamic-slice_convert_fusion.refs_0_), channel_id=1, source_target_pairs={{0,4},{2,6},{4,0},{6,2},{8,12},{10,14},{12,8},{14,10},{1,5},{3,7},... | collective-permute-start | bytes 196616 | tf_op jit(solution)/shard_map/ppermute | solution.py:243
  4.0 2.6 %collective-permute-start.1 = (u16[256,128]{1,0:T(8,128)(2,1)S(1)}, u16[256,128]{1,0:T(8,128)(2,1)S(1)}, u32[]{:S(2)}, u32[]{:S(2)}) collective-permute-start(u16[256,128]{1,0:T(8,128)(2,1)S(1)} %dynamic-slice_convert_fusion.refs_0_), channel_id=1, source_target_pairs={{0,8},{2,10},{4,12},{6,14},{8,0},{10,2},{12,4},{14,6},{1,9},{3,11}... | collective-permute-start | bytes 196616 | tf_op jit(solution)/shard_map/ppermute | solution.py:243
  6.6 0.0 collective-permute-start.2
  6.6 0.0 collective-permute-start.3
  6.6 1.6 %copy-done = bf16[4096,1,256]{2,0,1:T(8,128)(2,1)S(1)} copy-done((bf16[4096,1,256]{2,0,1:T(8,128)(2,1)S(1)}, bf16[4096,1,256]{2,0,1:T(8,128)(2,1)}, u32[]{:S(2)}) %copy-start) | copy-done | bytes 2097176
  8.2 0.1 fetch.1.own_ref
  8.4 0.0 collective-permute-done.3
  8.4 0.0 collective-permute-done.4.sib_ref
  8.4 4.6 %spread.2.refs_4_.refs_0_.refs_14_.refs_15_.refs_16_.refs_17_.refs_18_.refs_19_ = bf16[512,1024]{1,0:T(8,128)(2,1)S(1)} custom-call(s32[1,2048]{1,0:T(1,128)S(1)} %bitcast.17, bf16[4096,256]{1,0:T(8,128)(2,1)S(1)} %fetch.1.own_ref, s32[1,2048]{1,0:T(1,128)S(1)} %bitcast.19, bf16[4096,256]{1,0:T(8,128)(2,1)S(1)} %collective-permute-done.4.sib_ref), custom_call_target="tpu_custom_call" | custom-call | flops 134217728 | bytes 1048576 | tf_op jit(solution)/shard_map/spread/pallas_call | solution.py:123
  13.1 0.0 collective-permute-done.refs_1_
  13.1 0.0 collective-permute-done.1.refs_2_
  13.1 0.0 collective-permute-done.2.refs_3_
  13.1 1.1 %unpack.4 = (f8e4m3fn[1024,2048]{1,0:T(32,128)(4,1)S(1)}, f32[1024,128]{1,0:T(8,128)S(1)}, u16[4,256,128]{2,1,0:T(8,128)(2,1)S(1)}, u16[256,128]{1,0:T(8,128)(2,...) custom-call(u16[256,128]{1,0:T(8,128)(2,1)S(1)} %dynamic-slice_convert_fusion.refs_0_,, ...), custom_call_target="tpu_custom_call" | custom-call | flops 8589934592 | bytes 32768 | tf_op jit(solution)/shard_map/unpack/pallas_call | solution.py:52
  14.1 0.5 collective-permute-start.6
  14.7 1.7 %collective-permute-start.5 = (u16[4,256,128]{2,1,0:T(8,128)(2,1)S(1)}, u16[4,256,128]{2,1,0:T(8,128)(2,1)S(1)}, u32[]{:S(2)}, u32[]{:S(2)}) collective-permute-start(u16[4,256,128]{2,1,0:T(8,128)(2,1)S(1)} %get-tuple-element.54.refs_0_), channel_id=1, source_target_pairs={{0,2},{2,0},{4,6},{6,4},{8,10},{10,8},{12,14},{14,12},{1,3},{3,1},... | collective-permute-start | bytes 786440 | tf_op jit(solution)/shard_map/ppermute | solution.py:243
  16.4 0.0 collective-permute-start.7
  16.4 4.6 %spread.3.refs_1_ = bf16[512,1024]{1,0:T(8,128)(2,1)S(1)} custom-call(s32[1,2048]{1,0:T(1,128)S(1)} %bitcast.18, bf16[4096,256]{1,0:T(8,128)(2,1)S(1)} %fetch.1.own_ref, s32[1,2048]{1,0:T(1,128)S(1)} %bitcast.20, bf16[4096,256]{1,0:T(8,128)(2,1)S(1)} %collective-permute-done.4.sib_ref, u16[4,256,128]{2,1,0:T(8,128)(2,1)S(1)} %get-tuple-element.54.refs_0_), custom_call_target="tpu_custom_call" | custom-call | flops 134217728 | bytes 1048576 | tf_op jit(solution)/shard_map/spread/pallas_call | solution.py:123
  21.1 0.6 collective-permute-start.8
  21.7 0.0 collective-permute-done.6.refs_0_
  21.7 1.0 %unpack.5 = (f8e4m3fn[1024,2048]{1,0:T(32,128)(4,1)S(1)}, f32[1024,128]{1,0:T(8,128)S(1)}) custom-call(u16[4,256,128]{2,1,0:T(8,128)(2,1)S(1)} %collective-permute-done.6.refs_0_), custom_call_target="tpu_custom_call" | custom-call | flops 8589934592 | bytes 32768 | tf_op jit(solution)/shard_map/unpack/pallas_call | solution.py:52
  22.7 0.3 collective-permute-done.5.refs_0_
  23.0 0.0 collective-permute-start.9
  23.0 1.0 %unpack.6 = (f8e4m3fn[1024,2048]{1,0:T(32,128)(4,1)S(1)}, f32[1024,128]{1,0:T(8,128)S(1)}, u16[256,128]{1,0:T(8,128)(2,1)S(1)}, u16[256,128]{1,0:T(8,128)(2,1)S(...) custom-call(u16[4,256,128]{2,1,0:T(8,128)(2,1)S(1)} %collective-permute-done.5.refs_0_, ...), custom_call_target="tpu_custom_call" | custom-call | flops 8589934592 | bytes 32768 | tf_op jit(solution)/shard_map/unpack/pallas_call | solution.py:52
  24.0 0.5 collective-permute-done.9.refs_0_
  24.5 1.1 %unpack.7 = (f8e4m3fn[1024,2048]{1,0:T(32,128)(4,1)S(1)}, f32[1024,128]{1,0:T(8,128)S(1)}) custom-call(u16[4,256,128]{2,1,0:T(8,128)(2,1)S(1)} %collective-permute-done.9.refs_0_), custom_call_target="tpu_custom_call" | custom-call | flops 8589934592 | bytes 32768 | tf_op jit(solution)/shard_map/unpack/pallas_call | solution.py:52
  25.7 0.0 collective-permute-done.8.refs_3_
  25.7 3.8 %block.8 = (bf16[2,256,256]{2,1,0:T(8,128)(2,1)S(1)}, bf16[2,256,256]{2,1,0:T(8,128)(2,1)S(1)}, bf16[256,256]{1,0:T(8,128)(2,1)S(1)}, bf16[256,256]{1,0:T(8,128)(2,1)S(1)}) custom-call(u16[256,128]{1,0:T(8,128)(2,1)S(1)} %get-tuple-element.56.words_ref, bf16[512,1024]{1,0:T(8,128)(2,1)S(1)} %spread.2.refs_4_.refs_0_.refs_14_.refs_15_.refs_16_.refs_17_.refs_18_.refs_19_, ...), custom_call_target="tpu_custom_call" | custom-call | flops 5368709120 | bytes 65536 | tf_op jit(solution)/shard_map/block/pallas_call | solution.py:185
  29.5 4.8 %collective-permute-start.10 = (bf16[2,256,256]{2,1,0:T(8,128)(2,1)S(1)}, bf16[2,256,256]{2,1,0:T(8,128)(2,1)S(1)}, u32[]{:S(2)}, u32[]{:S(2)}) collective-permute-start(bf16[2,256,256]{2,1,0:T(8,128)(2,1)S(1)} %get-tuple-element.64.refs_15_), channel_id=1, source_target_pairs={{0,14},{2,12},{4,10},{6,8},{8,6},{10,4},{12,2},{14,0},{1,15},{3,13... | collective-permute-start | bytes 786440 | tf_op jit(solution)/shard_map/ppermute | solution.py:243
  34.3 3.8 %block.9 = (bf16[2,256,256]{2,1,0:T(8,128)(2,1)S(1)}, bf16[2,256,256]{2,1,0:T(8,128)(2,1)S(1)}, bf16[256,256]{1,0:T(8,128)(2,1)S(1)}, bf16[256,256]{1,0:T(8,128)(2,1)S(1)}) custom-call(u16[256,128]{1,0:T(8,128)(2,1)S(1)} %get-tuple-element.65.words_ref, bf16[512,1024]{1,0:T(8,128)(2,1)S(1)} %spread.2.refs_4_.refs_0_.refs_14_.refs_15_.refs_16_.refs_17_.refs_18_.refs_19_, ...), custom_call_target="tpu_custom_call" | custom-call | flops 5368709120 | bytes 65536 | tf_op jit(solution)/shard_map/block/pallas_call | solution.py:185
  38.1 0.3 collective-permute-start.12
  38.4 3.8 %block.10 = (bf16[2,256,256]{2,1,0:T(8,128)(2,1)S(1)}, bf16[2,256,256]{2,1,0:T(8,128)(2,1)S(1)}, bf16[256,256]{1,0:T(8,128)(2,1)S(1)}, bf16[256,256]{1,0:T(8,128)(2,1)S(1)}) custom-call(u16[256,128]{1,0:T(8,128)(2,1)S(1)} %get-tuple-element.71.words_ref, bf16[512,1024]{1,0:T(8,128)(2,1)S(1)} %spread.2.refs_4_.refs_0_.refs_14_.refs_15_.refs_16_.refs_17_.refs_18_.refs_19_, ...), custom_call_target="tpu_custom_call" | custom-call | flops 5368709120 | bytes 65536 | tf_op jit(solution)/shard_map/block/pallas_call | solution.py:185
  42.1 0.1 collective-permute-start.14
  42.2 4.0 %block.11 = (bf16[2,256,256]{2,1,0:T(8,128)(2,1)S(1)}, bf16[2,256,256]{2,1,0:T(8,128)(2,1)S(1)}, bf16[256,256]{1,0:T(8,128)(2,1)S(1)}, bf16[256,256]{1,0:T(8,128)(2,1)S(1)}) custom-call(u16[256,128]{1,0:T(8,128)(2,1)S(1)} %get-tuple-element.77.words_ref, bf16[512,1024]{1,0:T(8,128)(2,1)S(1)} %spread.2.refs_4_.refs_0_.refs_14_.refs_15_.refs_16_.refs_17_.refs_18_.refs_19_, ...), custom_call_target="tpu_custom_call" | custom-call | flops 5368709120 | bytes 65536 | tf_op jit(solution)/shard_map/block/pallas_call | solution.py:185
  46.2 0.1 collective-permute-start.16
  46.3 0.0 collective-permute-done.14.refs_13_
  46.3 3.8 %block.12 = (bf16[2,256,256]{2,1,0:T(8,128)(2,1)S(1)}, bf16[2,256,256]{2,1,0:T(8,128)(2,1)S(1)}, bf16[256,256]{1,0:T(8,128)(2,1)S(1)}, bf16[256,256]{1,0:T(8,128)(2,1)S(1)}) custom-call(u16[256,128]{1,0:T(8,128)(2,1)S(1)} %get-tuple-element.70.words_ref, bf16[512,1024]{1,0:T(8,128)(2,1)S(1)} %spread.2.refs_4_.refs_0_.refs_14_.refs_15_.refs_16_.refs_17_.refs_18_.refs_19_, ...), custom_call_target="tpu_custom_call" | custom-call | flops 5368709120 | bytes 65536 | tf_op jit(solution)/shard_map/block/pallas_call | solution.py:185
  50.1 5.1 %collective-permute-start.18 = (bf16[2,256,256]{2,1,0:T(8,128)(2,1)S(1)}, bf16[2,256,256]{2,1,0:T(8,128)(2,1)S(1)}, u32[]{:S(2)}, u32[]{:S(2)}) collective-permute-start(bf16[2,256,256]{2,1,0:T(8,128)(2,1)S(1)} %get-tuple-element.85.refs_15_), channel_id=1, source_target_pairs={{0,6},{2,4},{4,2},{6,0},{8,14},{10,12},{12,10},{14,8},{1,7},{3,5},... | collective-permute-start | bytes 786440 | tf_op jit(solution)/shard_map/ppermute | solution.py:243
  55.2 0.0 collective-permute-start.15
  55.2 0.0 collective-permute-done.10.refs_18_.refs_0_
  55.2 3.8 %block.13 = (bf16[2,256,256]{2,1,0:T(8,128)(2,1)S(1)}, bf16[2,256,256]{2,1,0:T(8,128)(2,1)S(1)}, bf16[256,256]{1,0:T(8,128)(2,1)S(1)}, bf16[256,256]{1,0:T(8,128)(2,1)S(1)}) custom-call(u16[256,128]{1,0:T(8,128)(2,1)S(1)} %get-tuple-element.86.words_ref, bf16[512,1024]{1,0:T(8,128)(2,1)S(1)} %spread.2.refs_4_.refs_0_.refs_14_.refs_15_.refs_16_.refs_17_.refs_18_.refs_19_, ...), custom_call_target="tpu_custom_call" | custom-call | flops 5368709120 | bytes 65536 | tf_op jit(solution)/shard_map/block/pallas_call | solution.py:185
  59.0 1.4 %collective-permute-start.20 = (bf16[2,256,256]{2,1,0:T(8,128)(2,1)S(1)}, bf16[2,256,256]{2,1,0:T(8,128)(2,1)S(1)}, u32[]{:S(2)}, u32[]{:S(2)}) collective-permute-start(bf16[2,256,256]{2,1,0:T(8,128)(2,1)S(1)} %get-tuple-element.89.refs_15_), channel_id=1, source_target_pairs={{0,4},{2,6},{4,0},{6,2},{8,12},{10,14},{12,8},{14,10},{1,5},{3,7},... | collective-permute-start | bytes 786440 | tf_op jit(solution)/shard_map/ppermute | solution.py:243
  60.3 0.0 collective-permute-done.12.refs_18_.refs_2_
  60.3 3.8 %block.14 = (bf16[2,256,256]{2,1,0:T(8,128)(2,1)S(1)}, bf16[2,256,256]{2,1,0:T(8,128)(2,1)S(1)}, bf16[256,256]{1,0:T(8,128)(2,1)S(1)}, bf16[256,256]{1,0:T(8,128)(2,1)S(1)}) custom-call(u16[256,128]{1,0:T(8,128)(2,1)S(1)} %get-tuple-element.90.words_ref, bf16[512,1024]{1,0:T(8,128)(2,1)S(1)} %spread.2.refs_4_.refs_0_.refs_14_.refs_15_.refs_16_.refs_17_.refs_18_.refs_19_, ...), custom_call_target="tpu_custom_call" | custom-call | flops 5368709120 | bytes 65536 | tf_op jit(solution)/shard_map/block/pallas_call | solution.py:185
  64.1 0.6 collective-permute-start.22
  64.7 3.8 %block.15 = (bf16[2,256,256]{2,1,0:T(8,128)(2,1)S(1)}, bf16[2,256,256]{2,1,0:T(8,128)(2,1)S(1)}, bf16[256,256]{1,0:T(8,128)(2,1)S(1)}, bf16[256,256]{1,0:T(8,128)(2,1)S(1)}) custom-call(u16[256,128]{1,0:T(8,128)(2,1)S(1)} %get-tuple-element.95.words_ref, bf16[512,1024]{1,0:T(8,128)(2,1)S(1)} %spread.2.refs_4_.refs_0_.refs_14_.refs_15_.refs_16_.refs_17_.refs_18_.refs_19_, ...), custom_call_target="tpu_custom_call" | custom-call | flops 5368709120 | bytes 65536 | tf_op jit(solution)/shard_map/block/pallas_call | solution.py:185
  68.5 5.3 %collective-permute-done.16.refs_6_ = bf16[2,256,256]{2,1,0:T(8,128)(2,1)S(1)} collective-permute-done((bf16[2,256,256]{2,1,0:T(8,128)(2,1)S(1)}, bf16[2,256,256]{2,1,0:T(8,128)(2,1)S(1)}, u32[]{:S(2)}, u32[]{:S(2)}) %collective-permute-start.16) | collective-permute-done | bytes 262176 | tf_op jit(solution)/shard_map/ppermute | solution.py:243
  73.7 0.0 collective-permute-start.24
  73.7 0.0 collective-permute-done.18.refs_8_
  73.7 0.6 collective-permute-start.17
  74.3 1.2 %collective-permute-done.22.refs_12_ = bf16[2,256,256]{2,1,0:T(8,128)(2,1)S(1)} collective-permute-done((bf16[2,256,256]{2,1,0:T(8,128)(2,1)S(1)}, bf16[2,256,256]{2,1,0:T(8,128)(2,1)S(1)}, u32[]{:S(2)}, u32[]{:S(2)}) %collective-permute-start.22) | collective-permute-done | bytes 262176 | tf_op jit(solution)/shard_map/ppermute | solution.py:243
  75.5 0.0 collective-permute-start.13
  75.6 0.0 collective-permute-done.20.refs_10_
  75.6 0.6 collective-permute-start.11
  76.2 0.0 collective-permute-done.24.refs_15_
  76.2 0.1 collective-permute-start.19
  76.3 2.3 %collective-permute-done.15.refs_4_.refs_5_ = bf16[2,256,256]{2,1,0:T(8,128)(2,1)S(1)} collective-permute-done((bf16[2,256,256]{2,1,0:T(8,128)(2,1)S(1)}, bf16[2,256,256]{2,1,0:T(8,128)(2,1)S(1)}, u32[]{:S(2)}, u32[]{:S(2)}) %collective-permute-start.15) | collective-permute-done | bytes 262176 | tf_op jit(solution)/shard_map/ppermute | solution.py:243
  78.5 0.5 collective-permute-start.21
  79.0 0.0 collective-permute-done.11.refs_1_
  79.1 0.0 collective-permute-done.19.refs_9_
  79.1 0.8 %collective-permute-done.23.refs_13_ = bf16[256,256]{1,0:T(8,128)(2,1)S(1)} collective-permute-done((bf16[256,256]{1,0:T(8,128)(2,1)S(1)}, bf16[256,256]{1,0:T(8,128)(2,1)S(1)}, u32[]{:S(2)}, u32[]{:S(2)}) %collective-permute-start.23) | collective-permute-done | bytes 131104 | tf_op jit(solution)/shard_map/ppermute | solution.py:246
  79.9 0.2 collective-permute-done.21.refs_11_
  80.1 1.6 %fill.1 = bf16[512,2048]{1,0:T(8,128)(2,1)} custom-call(bf16[2,256,256]{2,1,0:T(8,128)(2,1)S(1)} %collective-permute-done.10.refs_18_.refs_0_, bf16[256,256]{1,0:T(8,128)(2,1)S(1)} %collective-permute-done.11.refs_1_, bf16[2,256,256]{2,1,0:T(8,128)(2,1)S(1)} %collective-permute-done.12.refs_18_.refs_2_, ...), custom_call_target="tpu_custom_call" | custom-call | tf_op jit(solution)/shard_map/fill/pallas_call | solution.py:224
  (14 shorter events, 0.1 us)
Async XLA Ops:
  0.0 8.4 %collective-permute-start.4 = (bf16[4096,256]{1,0:T(8,128)(2,1)}, bf16[4096,256]{1,0:T(8,128)(2,1)S(1)}, u32[]{:S(2)}, u32[]{:S(2)}) collective-permute-start(bf16[4096,256]{1,0:T(8,128)(2,1)} %bitcast.15), channel_id=1, source_target_pairs={{0,1},{1,0},{2,3},{3,2},{4,5},{5,4},{6,7},{7,6},{8,9},{9,8},{10,11... | collective-permute-start | bytes 6291464 | tf_op jit(solution)/shard_map/ppermute | solution.py:246
  0.5 7.9 %copy-start.1 = (s32[2048]{0:T(1024)S(1)}, s32[2048]{0:T(1024)}, u32[]{:S(2)}) copy-start(s32[2048]{0:T(1024)} %param.4) | copy-start | bytes 24580
  1.4 11.7 %collective-permute-start = (u16[256,128]{1,0:T(8,128)(2,1)S(1)}, u16[256,128]{1,0:T(8,128)(2,1)S(1)}, u32[]{:S(2)}, u32[]{:S(2)}) collective-permute-start(u16[256,128]{1,0:T(8,128)(2,1)S(1)} %dynamic-slice_convert_fusion.refs_0_), channel_id=1, source_target_pairs={{0,4},{2,6},{4,0},{6,2},{8,12},{10,14},{12,8},{14,10},{1,5},{3,7},... | collective-permute-start | bytes 196616 | tf_op jit(solution)/shard_map/ppermute | solution.py:243
  4.0 9.0 %collective-permute-start.1 = (u16[256,128]{1,0:T(8,128)(2,1)S(1)}, u16[256,128]{1,0:T(8,128)(2,1)S(1)}, u32[]{:S(2)}, u32[]{:S(2)}) collective-permute-start(u16[256,128]{1,0:T(8,128)(2,1)S(1)} %dynamic-slice_convert_fusion.refs_0_), channel_id=1, source_target_pairs={{0,8},{2,10},{4,12},{6,14},{8,0},{10,2},{12,4},{14,6},{1,9},{3,11}... | collective-permute-start | bytes 196616 | tf_op jit(solution)/shard_map/ppermute | solution.py:243
  6.6 6.5 %collective-permute-start.2 = (u16[256,128]{1,0:T(8,128)(2,1)S(1)}, u16[256,128]{1,0:T(8,128)(2,1)S(1)}, u32[]{:S(2)}, u32[]{:S(2)}) collective-permute-start(u16[256,128]{1,0:T(8,128)(2,1)S(1)} %dynamic-slice_convert_fusion.refs_0_), channel_id=1, source_target_pairs={{0,12},{2,14},{4,8},{6,10},{8,4},{10,6},{12,0},{14,2},{1,13},{3,15... | collective-permute-start | bytes 196616 | tf_op jit(solution)/shard_map/ppermute | solution.py:243
  6.6 1.8 %collective-permute-start.3 = (s32[2048]{0:T(1024)}, s32[2048]{0:T(1024)S(1)}, u32[]{:S(2)}, u32[]{:S(2)}) collective-permute-start(s32[2048]{0:T(1024)} %param.4), channel_id=1, source_target_pairs={{0,1},{1,0},{2,3},{3,2},{4,5},{5,4},{6,7},{7,6},{8,9},{9,8},{10,11... | collective-permute-start | bytes 24584 | tf_op jit(solution)/shard_map/ppermute | solution.py:246
  6.6 1.6 %copy-start = (bf16[4096,1,256]{2,0,1:T(8,128)(2,1)S(1)}, bf16[4096,1,256]{2,0,1:T(8,128)(2,1)}, u32[]{:S(2)}) copy-start(bf16[4096,1,256]{2,0,1:T(8,128)(2,1)} %param.5) | copy-start | bytes 6291460
  14.1 7.5 %collective-permute-start.6 = (u16[4,256,128]{2,1,0:T(8,128)(2,1)S(1)}, u16[4,256,128]{2,1,0:T(8,128)(2,1)S(1)}, u32[]{:S(2)}, u32[]{:S(2)}) collective-permute-start(u16[4,256,128]{2,1,0:T(8,128)(2,1)S(1)} %get-tuple-element.54.refs_0_), channel_id=1, source_target_pairs={{0,1},{1,0},{2,3},{3,2},{4,5},{5,4},{6,7},{7,6},{8,9},{9,8},{10,11... | collective-permute-start | bytes 786440 | tf_op jit(solution)/shard_map/ppermute | solution.py:246
  14.7 8.3 %collective-permute-start.5 = (u16[4,256,128]{2,1,0:T(8,128)(2,1)S(1)}, u16[4,256,128]{2,1,0:T(8,128)(2,1)S(1)}, u32[]{:S(2)}, u32[]{:S(2)}) collective-permute-start(u16[4,256,128]{2,1,0:T(8,128)(2,1)S(1)} %get-tuple-element.54.refs_0_), channel_id=1, source_target_pairs={{0,2},{2,0},{4,6},{6,4},{8,10},{10,8},{12,14},{14,12},{1,3},{3,1},... | collective-permute-start | bytes 786440 | tf_op jit(solution)/shard_map/ppermute | solution.py:243
  16.4 9.3 %collective-permute-start.7 = (bf16[512,1024]{1,0:T(8,128)(2,1)S(1)}, bf16[512,1024]{1,0:T(8,128)(2,1)S(1)}, u32[]{:S(2)}, u32[]{:S(2)}) collective-permute-start(bf16[512,1024]{1,0:T(8,128)(2,1)S(1)} %spread.2.refs_4_.refs_0_.refs_14_.refs_15_.refs_16_.refs_17_.refs_18_.refs_19_), channel_id=1, source_target_pairs={{0,1},{1,0},{2,3},{3,2},{4,5},{5,4},{6,7},{7,6},{8,9},{9,8},{10,11... | collective-permute-start | bytes 3145736 | tf_op jit(solution)/shard_map/ppermute | solution.py:246
  21.1 4.6 %collective-permute-start.8 = (bf16[512,1024]{1,0:T(8,128)(2,1)S(1)}, bf16[512,1024]{1,0:T(8,128)(2,1)S(1)}, u32[]{:S(2)}, u32[]{:S(2)}) collective-permute-start(bf16[512,1024]{1,0:T(8,128)(2,1)S(1)} %spread.3.refs_1_), channel_id=1, source_target_pairs={{0,1},{1,0},{2,3},{3,2},{4,5},{5,4},{6,7},{7,6},{8,9},{9,8},{10,11... | collective-permute-start | bytes 3145736 | tf_op jit(solution)/shard_map/ppermute | solution.py:246
  23.0 1.5 %collective-permute-start.9 = (u16[4,256,128]{2,1,0:T(8,128)(2,1)S(1)}, u16[4,256,128]{2,1,0:T(8,128)(2,1)S(1)}, u32[]{:S(2)}, u32[]{:S(2)}) collective-permute-start(u16[4,256,128]{2,1,0:T(8,128)(2,1)S(1)} %collective-permute-done.5.refs_0_), channel_id=1, source_target_pairs={{0,1},{1,0},{2,3},{3,2},{4,5},{5,4},{6,7},{7,6},{8,9},{9,8},{10,11... | collective-permute-start | bytes 786440 | tf_op jit(solution)/shard_map/ppermute | solution.py:246
  29.5 25.7 %collective-permute-start.10 = (bf16[2,256,256]{2,1,0:T(8,128)(2,1)S(1)}, bf16[2,256,256]{2,1,0:T(8,128)(2,1)S(1)}, u32[]{:S(2)}, u32[]{:S(2)}) collective-permute-start(bf16[2,256,256]{2,1,0:T(8,128)(2,1)S(1)} %get-tuple-element.64.refs_15_), channel_id=1, source_target_pairs={{0,14},{2,12},{4,10},{6,8},{8,6},{10,4},{12,2},{14,0},{1,15},{3,13... | collective-permute-start | bytes 786440 | tf_op jit(solution)/shard_map/ppermute | solution.py:243
  38.1 22.2 %collective-permute-start.12 = (bf16[2,256,256]{2,1,0:T(8,128)(2,1)S(1)}, bf16[2,256,256]{2,1,0:T(8,128)(2,1)S(1)}, u32[]{:S(2)}, u32[]{:S(2)}) collective-permute-start(bf16[2,256,256]{2,1,0:T(8,128)(2,1)S(1)} %get-tuple-element.69.refs_15_), channel_id=1, source_target_pairs={{0,12},{2,14},{4,8},{6,10},{8,4},{10,6},{12,0},{14,2},{1,13},{3,15... | collective-permute-start | bytes 786440 | tf_op jit(solution)/shard_map/ppermute | solution.py:243
  42.1 4.2 %collective-permute-start.14 = (bf16[256,256]{1,0:T(8,128)(2,1)S(1)}, bf16[256,256]{1,0:T(8,128)(2,1)S(1)}, u32[]{:S(2)}, u32[]{:S(2)}) collective-permute-start(bf16[256,256]{1,0:T(8,128)(2,1)S(1)} %get-tuple-element.76.refs_13_.refs_17_), channel_id=1, source_target_pairs={{0,1},{1,0},{2,3},{3,2},{4,5},{5,4},{6,7},{7,6},{8,9},{9,8},{10,11... | collective-permute-start | bytes 393224 | tf_op jit(solution)/shard_map/ppermute | solution.py:246
  46.2 27.5 %collective-permute-start.16 = (bf16[2,256,256]{2,1,0:T(8,128)(2,1)S(1)}, bf16[2,256,256]{2,1,0:T(8,128)(2,1)S(1)}, u32[]{:S(2)}, u32[]{:S(2)}) collective-permute-start(bf16[2,256,256]{2,1,0:T(8,128)(2,1)S(1)} %get-tuple-element.81.refs_15_), channel_id=1, source_target_pairs={{0,10},{2,8},{4,14},{6,12},{8,2},{10,0},{12,6},{14,4},{1,11},{3,9}... | collective-permute-start | bytes 786440 | tf_op jit(solution)/shard_map/ppermute | solution.py:243
  50.1 23.7 %collective-permute-start.18 = (bf16[2,256,256]{2,1,0:T(8,128)(2,1)S(1)}, bf16[2,256,256]{2,1,0:T(8,128)(2,1)S(1)}, u32[]{:S(2)}, u32[]{:S(2)}) collective-permute-start(bf16[2,256,256]{2,1,0:T(8,128)(2,1)S(1)} %get-tuple-element.85.refs_15_), channel_id=1, source_target_pairs={{0,6},{2,4},{4,2},{6,0},{8,14},{10,12},{12,10},{14,8},{1,7},{3,5},... | collective-permute-start | bytes 786440 | tf_op jit(solution)/shard_map/ppermute | solution.py:243
  55.2 23.4 %collective-permute-start.15 = (bf16[2,256,256]{2,1,0:T(8,128)(2,1)S(1)}, bf16[2,256,256]{2,1,0:T(8,128)(2,1)S(1)}, u32[]{:S(2)}, u32[]{:S(2)}) collective-permute-start(bf16[2,256,256]{2,1,0:T(8,128)(2,1)S(1)} %get-tuple-element.84.refs_14_.refs_19_), channel_id=1, source_target_pairs={{0,8},{2,10},{4,12},{6,14},{8,0},{10,2},{12,4},{14,6},{1,9},{3,11}... | collective-permute-start | bytes 786440 | tf_op jit(solution)/shard_map/ppermute | solution.py:243
  59.0 16.6 %collective-permute-start.20 = (bf16[2,256,256]{2,1,0:T(8,128)(2,1)S(1)}, bf16[2,256,256]{2,1,0:T(8,128)(2,1)S(1)}, u32[]{:S(2)}, u32[]{:S(2)}) collective-permute-start(bf16[2,256,256]{2,1,0:T(8,128)(2,1)S(1)} %get-tuple-element.89.refs_15_), channel_id=1, source_target_pairs={{0,4},{2,6},{4,0},{6,2},{8,12},{10,14},{12,8},{14,10},{1,5},{3,7},... | collective-permute-start | bytes 786440 | tf_op jit(solution)/shard_map/ppermute | solution.py:243
  64.1 11.5 %collective-permute-start.22 = (bf16[2,256,256]{2,1,0:T(8,128)(2,1)S(1)}, bf16[2,256,256]{2,1,0:T(8,128)(2,1)S(1)}, u32[]{:S(2)}, u32[]{:S(2)}) collective-permute-start(bf16[2,256,256]{2,1,0:T(8,128)(2,1)S(1)} %get-tuple-element.94.refs_15_), channel_id=1, source_target_pairs={{0,2},{2,0},{4,6},{6,4},{8,10},{10,8},{12,14},{14,12},{1,3},{3,1},... | collective-permute-start | bytes 786440 | tf_op jit(solution)/shard_map/ppermute | solution.py:243
  73.7 2.4 %collective-permute-start.24 = (bf16[256,256]{1,0:T(8,128)(2,1)S(1)}, bf16[256,256]{1,0:T(8,128)(2,1)S(1)}, u32[]{:S(2)}, u32[]{:S(2)}) collective-permute-start(bf16[256,256]{1,0:T(8,128)(2,1)S(1)} %get-tuple-element.100), channel_id=1, source_target_pairs={{0,1},{1,0},{2,3},{3,2},{4,5},{5,4},{6,7},{7,6},{8,9},{9,8},{10,11... | collective-permute-start | bytes 393224 | tf_op jit(solution)/shard_map/ppermute | solution.py:246
  73.7 4.8 %collective-permute-start.17 = (bf16[256,256]{1,0:T(8,128)(2,1)S(1)}, bf16[256,256]{1,0:T(8,128)(2,1)S(1)}, u32[]{:S(2)}, u32[]{:S(2)}) collective-permute-start(bf16[256,256]{1,0:T(8,128)(2,1)S(1)} %slice_bitcast_fusion.3), channel_id=1, source_target_pairs={{0,1},{1,0},{2,3},{3,2},{4,5},{5,4},{6,7},{7,6},{8,9},{9,8},{10,11... | collective-permute-start | bytes 393224 | tf_op jit(solution)/shard_map/ppermute | solution.py:246
  75.5 3.5 %collective-permute-start.13 = (bf16[256,256]{1,0:T(8,128)(2,1)S(1)}, bf16[256,256]{1,0:T(8,128)(2,1)S(1)}, u32[]{:S(2)}, u32[]{:S(2)}) collective-permute-start(bf16[256,256]{1,0:T(8,128)(2,1)S(1)} %slice_bitcast_fusion.4), channel_id=1, source_target_pairs={{0,1},{1,0},{2,3},{3,2},{4,5},{5,4},{6,7},{7,6},{8,9},{9,8},{10,11... | collective-permute-start | bytes 393224 | tf_op jit(solution)/shard_map/ppermute | solution.py:246
  75.6 3.5 %collective-permute-start.11 = (bf16[256,256]{1,0:T(8,128)(2,1)S(1)}, bf16[256,256]{1,0:T(8,128)(2,1)S(1)}, u32[]{:S(2)}, u32[]{:S(2)}) collective-permute-start(bf16[256,256]{1,0:T(8,128)(2,1)S(1)} %slice_bitcast_fusion.5), channel_id=1, source_target_pairs={{0,1},{1,0},{2,3},{3,2},{4,5},{5,4},{6,7},{7,6},{8,9},{9,8},{10,11... | collective-permute-start | bytes 393224 | tf_op jit(solution)/shard_map/ppermute | solution.py:246
  76.2 2.9 %collective-permute-start.19 = (bf16[256,256]{1,0:T(8,128)(2,1)S(1)}, bf16[256,256]{1,0:T(8,128)(2,1)S(1)}, u32[]{:S(2)}, u32[]{:S(2)}) collective-permute-start(bf16[256,256]{1,0:T(8,128)(2,1)S(1)} %slice_bitcast_fusion.2), channel_id=1, source_target_pairs={{0,1},{1,0},{2,3},{3,2},{4,5},{5,4},{6,7},{7,6},{8,9},{9,8},{10,11... | collective-permute-start | bytes 393224 | tf_op jit(solution)/shard_map/ppermute | solution.py:246
  78.5 1.3 %collective-permute-start.23 = (bf16[256,256]{1,0:T(8,128)(2,1)S(1)}, bf16[256,256]{1,0:T(8,128)(2,1)S(1)}, u32[]{:S(2)}, u32[]{:S(2)}) collective-permute-start(bf16[256,256]{1,0:T(8,128)(2,1)S(1)} %slice_bitcast_fusion), channel_id=1, source_target_pairs={{0,1},{1,0},{2,3},{3,2},{4,5},{5,4},{6,7},{7,6},{8,9},{9,8},{10,11... | collective-permute-start | bytes 393224 | tf_op jit(solution)/shard_map/ppermute | solution.py:246
  78.5 1.5 %collective-permute-start.21 = (bf16[256,256]{1,0:T(8,128)(2,1)S(1)}, bf16[256,256]{1,0:T(8,128)(2,1)S(1)}, u32[]{:S(2)}, u32[]{:S(2)}) collective-permute-start(bf16[256,256]{1,0:T(8,128)(2,1)S(1)} %slice_bitcast_fusion.1), channel_id=1, source_target_pairs={{0,1},{1,0},{2,3},{3,2},{4,5},{5,4},{6,7},{7,6},{8,9},{9,8},{10,11... | collective-permute-start | bytes 393224 | tf_op jit(solution)/shard_map/ppermute | solution.py:246
